TPU v7x, 256 devices: a whole 4x4x8 slice. The times are simulated.
256 devices in a mesh: gx: 32 (over z, x), gy: 8 (over y, core).
Axes of the slice: x: 4, y: 4, z: 8, core: 2. Of those that a mesh axis runs over, the one named last changes fastest.
Arguments:
- leaf_multipoles: float32 [64, 128, 64, 128], P(None, 'gx', 'gy'), may hold values from -6 to 6
- m2l_ops: bfloat16 [316, 32, 32], replicated, may hold values from -0.078125 to 0.078125
- proj_in: float32 [32, 64], replicated, may hold values from -0.75 to 0.75
- proj_out: float32 [64, 32], replicated, may hold values from -1 to 1
- m2m: float32 [8, 64, 64], replicated, may hold values from -0.75 to 0.75
Outputs:
- leaf_locals: float32 [64, 128, 64, 128], P(None, 'gx', 'gy')
All inputs are finite; a program needn't handle non-finite values.
Results may differ from a plain program's by a relative error of at most 0.0029.
Values may be sent and summed in bfloat16 or wider, within the bound.
A program may use at most 128 MiB of HBM per device.

v0:
```python
import functools

import jax
import jax.numpy as jnp
from jax import lax
from jax.experimental import pallas as pl
from jax.experimental.pallas import tpu as pltpu
from jax.sharding import PartitionSpec as P

MESH = pl.DeviceIdType.MESH
F32 = jnp.float32
BF16 = jnp.bfloat16
NT = (((1,), (1,)), ((), ()))


def dot_nt(a, b):
    return lax.dot_general(a, b, NT, preferred_element_type=F32)


def split(value):
    high = value.astype(BF16)
    return high, (value - high.astype(F32)).astype(BF16)


def dot3(a_high, a_low, b_high, b_low):
    return dot_nt(a_high, b_high) + (dot_nt(a_low, b_high) + dot_nt(a_high, b_low))


def lanes(shape):
    return lax.broadcasted_iota(jnp.int32, shape, 1)


def rows(shape):
    return lax.broadcasted_iota(jnp.int32, shape, 0)


def hole_runs():
    runs, first, number = [], 0, 0
    position = 0
    for ox in range(-3, 4):
        for oy in range(-3, 4):
            for oz in range(-3, 4):
                near = max(abs(ox), abs(oy), abs(oz)) < 2
                if not near:
                    if runs and runs[-1][0] + runs[-1][2] == position:
                        runs[-1][2] += 1
                    else:
                        runs.append([position, number, 1])
                    number += 1
                position += 1
    return runs


RUNS = hole_runs()
NEIGHBOURS = [(1, 0), (-1, 0), (0, 1), (0, -1), (1, 1), (1, -1), (-1, 1), (-1, -1)]


def kernel(
    n_gx, n_gy,
    x_hbm, ops_hbm, pin_ref, pout_ref, m2m_ref,
    out_ref,
    x_ref, ops_ref, turn_ref, dh_ref, dl_ref, m1_ref, m2_ref, src0, src1, cin, cout, rep_ref, q_ref,
    wup_ref, wd_ref, far_ref, h_ref, l1_ref,
    in_sem, ops_sem, send0, recv0, send1, recv1, send2, recv2,
):
    px, py = lax.axis_index("gx"), lax.axis_index("gy")
    parity = lax.rem(px, 2)

    def device(dx, dy):
        return (lax.rem(px + (dx + n_gx), n_gx), lax.rem(py + (dy + n_gy), n_gy))

    far_dx = 3 - 6 * parity
    coarse_moves = [
        (dx, dy) for dx in (0, 1, -1, 2, -2, None) for dy in (0, 1, -1) if (dx, dy) != (0, 0)
    ]
    coarse_moves = [(far_dx if dx is None else dx, dy) for dx, dy in coarse_moves]

    barrier = pltpu.get_barrier_semaphore()
    for dx, dy in coarse_moves:
        pl.semaphore_signal(barrier, inc=1, device_id=device(dx, dy), device_id_type=MESH)

    x_copy = pltpu.make_async_copy(x_hbm, x_ref, in_sem)
    x_copy.start()
    ops_copies = []
    for k, (position, number, count) in enumerate(RUNS):
        copy = pltpu.make_async_copy(
            ops_hbm.at[pl.ds(number, count)], ops_ref.at[pl.ds(position, count)], ops_sem.at[k]
        )
        copy.start()
        ops_copies.append(copy)
    for ox in (2, 3, 4):
        for oy in (2, 3, 4):
            ops_ref[pl.ds((ox * 7 + oy) * 7 + 2, 3)] = jnp.zeros((3, 32, 32), BF16)

    pin = pin_ref[...]
    pin2 = jnp.concatenate([pin, pin], axis=1)
    pin4 = jnp.concatenate([pin2, pin2], axis=1)
    pack = jnp.concatenate([pin4, pin4, pin4, pin4], axis=0)
    pack = jnp.where(rows(pack.shape) // 32 == lanes(pack.shape) // 64, pack, 0.0)
    for sz in range(2):
        mix = jnp.concatenate([m2m_ref[2 * s + sz] for s in range(4)], axis=1)
        high, low = split(jnp.concatenate([pack, mix], axis=0))
        wup_ref[sz, 0] = high
        wup_ref[sz, 1] = low
    pout = pout_ref[...]
    pout2 = jnp.concatenate([pout, pout], axis=1)
    pout4 = jnp.concatenate([pout2, pout2], axis=1)
    unpack = jnp.concatenate([pout4, pout4, pout4, pout4], axis=0)
    unpack = jnp.where(rows(unpack.shape) // 64 == lanes(unpack.shape) // 32, unpack, 0.0)
    down = jnp.concatenate([m2m_ref[2 * s : 2 * s + 2].reshape(128, 64).T for s in range(4)], axis=0)
    high, low = split(jnp.concatenate([unpack, down], axis=1))
    wd_ref[0] = high
    wd_ref[1] = low

    x_copy.wait()

    for X in range(2):
        for Y in range(4):
            parent = X * 4 + Y
            block = jnp.concatenate(
                [
                    x_ref[pl.ds((2 * X + sx) * 8 + 2 * Y + sy, 64, stride=32), :]
                    for sx in range(2)
                    for sy in range(2)
                ],
                axis=0,
            )
            turned = block.T
            turn_ref[parent, 0] = turned[:, :128]
            turn_ref[parent, 1] = turned[:, 128:]
            for sz in range(2):
                high, low = split(
                    jnp.concatenate(
                        [turn_ref[parent, sx, pl.ds(sz, 64, stride=2), :] for sx in range(2)], axis=1
                    )
                )
                dh_ref[sz, pl.ds(parent * 64, 64)] = high
                dl_ref[sz, pl.ds(parent * 64, 64)] = low
    total = None
    for sz in range(2):
        made = dot3(dh_ref[sz], dl_ref[sz], wup_ref[sz, 0], wup_ref[sz, 1])
        src0[1:3, 1:5, :, sz * 128 : (sz + 1) * 128] = made[:, :128].astype(BF16).reshape(2, 4, 64, 128)
        total = made[:, 128:] if sz == 0 else total + made[:, 128:]
    m1_ref[:, 0:64] = total

    total = None
    for sz in range(2):
        block = jnp.concatenate(
            [
                jnp.concatenate(
                    [
                        m1_ref[pl.ds((sx * 4 + 2 * Y1 + sy) * 64 + sz, 32, stride=2), :][:, 0:64]
                        for sx in range(2)
                        for sy in range(2)
                    ],
                    axis=1,
                )
                for Y1 in range(2)
            ],
            axis=0,
        )
        high, low = split(block)
        made = dot3(high, low, wup_ref[sz, 0], wup_ref[sz, 1])
        src1[1, 1:3, :, sz * 128 : (sz + 1) * 128] = made[:, :128].astype(BF16).reshape(2, 32, 128)
        total = made[:, 128:] if sz == 0 else total + made[:, 128:]
    m2_ref[:, 0:64] = total

    for sz in range(2):
        pair = jnp.concatenate([m2_ref[pl.ds(sy * 32 + sz, 16, stride=2), :][:, 0:64] for sy in range(2)], axis=1)
        block = jnp.concatenate([pair, pair], axis=1)
        block = jnp.where(lanes(block.shape) // 128 == parity, block, 0.0)
        high, low = split(block)
        made = dot3(high, low, wup_ref[sz, 0, 0:128], wup_ref[sz, 1, 0:128])
        cout[:, sz * 128 : (sz + 1) * 128] = made.astype(BF16)

    pl.semaphore_wait(barrier, len(coarse_moves))

    copies = []
    for k, (dx, dy) in enumerate(NEIGHBOURS):
        for buffer, size_x, size_y, sends, recvs in ((src0, 2, 4, send0, recv0), (src1, 1, 2, send1, recv1)):
            from_x = {0: pl.ds(1, size_x), 1: pl.ds(size_x, 1), -1: pl.ds(1, 1)}[dx]
            from_y = {0: pl.ds(1, size_y), 1: pl.ds(size_y, 1), -1: pl.ds(1, 1)}[dy]
            to_x = {0: pl.ds(1, size_x), 1: pl.ds(0, 1), -1: pl.ds(size_x + 1, 1)}[dx]
            to_y = {0: pl.ds(1, size_y), 1: pl.ds(0, 1), -1: pl.ds(size_y + 1, 1)}[dy]
            copy = pltpu.make_async_remote_copy(
                src_ref=buffer.at[from_x, from_y],
                dst_ref=buffer.at[to_x, to_y],
                send_sem=sends.at[k],
                recv_sem=recvs.at[k],
                device_id=device(dx, dy),
                device_id_type=MESH,
            )
            copy.start()
            copies.append(copy)
    coarse_copies = []
    for k, (dx, dy) in enumerate(coarse_moves):
        to_parity = lax.rem(px + (dx + n_gx), 2)
        slot = (2 - dx) + to_parity
        copy = pltpu.make_async_remote_copy(
            src_ref=cout,
            dst_ref=cin.at[slot, 1 - dy],
            send_sem=send2.at[k],
            recv_sem=recv2.at[slot, 1 - dy],
            device_id=device(dx, dy),
            device_id_type=MESH,
        )
        copy.start()
        coarse_copies.append(copy)
    cin[2 + parity, 1] = cout[...]

    for copy in ops_copies:
        copy.wait()
    spread = jnp.where(lanes((32, 128)) % 32 == rows((32, 128)), 1.0, 0.0).astype(BF16)

    def replicate(k, _):
        blocks = ops_ref[pl.ds(k * 7, 7)].reshape(224, 32)
        made = jnp.dot(blocks, spread, preferred_element_type=F32).astype(BF16)
        rep_ref[k] = made.reshape(7, 32, 128)
        return 0

    lax.fori_loop(0, 49, replicate, 0)
    place = lanes((224, 128)) // 32

    def assemble(k, _):
        mx, my = k // 3, k % 3
        for tx in range(2):
            for ty in range(2):
                def piece(sx, sy):
                    return rep_ref[(2 * mx + 1 + sx - tx) * 7 + 2 * my + 1 + sy - ty].reshape(224, 128)

                upper = jnp.where(place == 0, piece(0, 0), piece(0, 1))
                lower = jnp.where(place == 2, piece(1, 0), piece(1, 1))
                made = jnp.where(place < 2, upper, lower)
                q_ref[mx, my, :, (2 * tx + ty) * 32 : (2 * tx + ty) * 32 + 32] = made.reshape(7, 32, 128)
        return 0

    lax.fori_loop(0, 9, assemble, 0)

    for copy in copies:
        copy.wait()
    for k, (dx, dy) in enumerate(coarse_moves):
        coarse_copies[k].wait_send()
        slot = dx + 2 + parity
        pltpu.make_async_remote_copy(
            src_ref=cout,
            dst_ref=cin.at[slot, 1 + dy],
            send_sem=send2.at[k],
            recv_sem=recv2.at[slot, 1 + dy],
            device_id=device(dx, dy),
            device_id_type=MESH,
        ).wait_recv()

    @pl.when(px == 0)
    def _():
        src0[0] = jnp.zeros(src0.shape[1:], BF16)
        src1[0] = jnp.zeros(src1.shape[1:], BF16)

    @pl.when(px == n_gx - 1)
    def _():
        src0[3] = jnp.zeros(src0.shape[1:], BF16)
        src1[2] = jnp.zeros(src1.shape[1:], BF16)

    @pl.when(py == 0)
    def _():
        src0[:, 0] = jnp.zeros((4, 64, 256), BF16)
        src1[:, 0] = jnp.zeros((3, 32, 256), BF16)

    @pl.when(py == n_gy - 1)
    def _():
        src0[:, 5] = jnp.zeros((4, 64, 256), BF16)
        src1[:, 3] = jnp.zeros((3, 32, 256), BF16)

    acc = None
    sums = []
    for mz in range(3):
        acc = None
        for mx in range(3):
            for my in range(3):
                parent_x, parent_y = px // 2 + mx - 1, py + my - 1
                inside = (parent_x >= 0) & (parent_x < n_gx // 2) & (parent_y >= 0) & (parent_y < n_gy)
                coarse = cin[2 * mx, my] + cin[2 * mx + 1, my]
                coarse = jnp.where(inside, coarse, jnp.zeros_like(coarse))
                source = jnp.concatenate(
                    [
                        src0[mx : mx + 2, my : my + 4].reshape(512, 256),
                        src1[mx, my : my + 2].reshape(64, 256),
                        coarse,
                    ],
                    axis=0,
                )
                weight = jnp.concatenate(
                    [
                        q_ref[mx, my, 2 * mz : 2 * mz + 2].reshape(256, 128),
                        q_ref[mx, my, 2 * mz + 1 : 2 * mz + 3].reshape(256, 128),
                    ],
                    axis=1,
                )
                made = dot_nt(source, weight)
                acc = made if acc is None else acc + made
        sums.append(acc)
    row = rows((592, 256))
    size = jnp.where(row < 512, 64, jnp.where(row < 576, 32, 16))
    inner = row & (size - 1)
    below = jnp.where(inner == 0, 0.0, pltpu.roll(sums[0], 1, 0))
    above = jnp.where(inner == size - 1, 0.0, pltpu.roll(sums[2], 591, 0))
    far_ref[...] = sums[1] + below + above

    wd_high, wd_low = wd_ref[0], wd_ref[1]
    twice_high = jnp.concatenate([wd_high[k * 64 : k * 64 + 64] for k in (0, 0, 1, 1, 2, 2, 3, 3)], axis=0)
    twice_low = jnp.concatenate([wd_low[k * 64 : k * 64 + 64] for k in (0, 0, 1, 1, 2, 2, 3, 3)], axis=0)

    for tz in range(2):
        part = slice(128, 256) if tz == 0 else slice(0, 128)
        h_ref[0, 0, pl.ds(tz, 16, stride=2), :] = far_ref[576:592, part] * 0.25
        for Y1 in range(2):
            h_ref[1, 0, pl.ds(Y1 * 64 + tz, 32, stride=2), :] = far_ref[512 + Y1 * 32 : 544 + Y1 * 32, part] * 0.5
    high, low = split(h_ref[0, 0, 0:32, :])
    made = dot3(high, low, twice_high[:, :128], twice_low[:, :128])
    local2 = jnp.where(parity == 1, made[:, 256:512], made[:, 0:256])
    half = lanes((32, 128)) // 64
    for Y1 in range(2):
        for tz in range(2):
            part = jnp.where(half == tz, local2[:, Y1 * 128 : Y1 * 128 + 128], 0.0)
            h_ref[1, 1, pl.ds(Y1 * 64 + tz, 32, stride=2), :] = part
    high, low = split(jnp.concatenate([h_ref[1, 0], h_ref[1, 1]], axis=1))
    l1_ref[...] = dot3(high, low, twice_high, twice_low)
    half = lanes((64, 128)) // 64
    for X in range(2):
        for Y in range(4):
            parent = X * 4 + Y
            here = h_ref.at[2 + parent]
            local = l1_ref[(Y // 2) * 64 : (Y // 2) * 64 + 64, (X * 2 + Y % 2) * 128 : (X * 2 + Y % 2) * 128 + 128]
            for tz in range(2):
                part = slice(128, 256) if tz == 0 else slice(0, 128)
                here[0, pl.ds(tz, 64, stride=2), :] = far_ref[parent * 64 : parent * 64 + 64, part]
                here[1, pl.ds(tz, 64, stride=2), :] = jnp.where(half == tz, local, 0.0)
            high, low = split(jnp.concatenate([here[0], here[1]], axis=1))
            made = dot3(wd_high, wd_low, high, low)
            for tx in range(2):
                for ty in range(2):
                    piece = made[(2 * tx + ty) * 64 : (2 * tx + ty) * 64 + 64]
                    out_ref[pl.ds((2 * X + tx) * 8 + 2 * Y + ty, 64, stride=32), :] = piece


def per_device(leaf_multipoles, m2l_ops, proj_in, proj_out, m2m, n_gx, n_gy):
    vmem = pl.BlockSpec(memory_space=pltpu.VMEM)
    hbm = pl.BlockSpec(memory_space=pl.ANY)
    made = pl.pallas_call(
        functools.partial(kernel, n_gx, n_gy),
        out_shape=jax.ShapeDtypeStruct((2048, 128), F32),
        in_specs=[hbm, hbm, vmem, vmem, vmem],
        out_specs=vmem,
        scratch_shapes=[
            pltpu.VMEM((2048, 128), F32),
            pltpu.VMEM((343, 32, 32), BF16),
            pltpu.VMEM((8, 2, 128, 128), F32),
            pltpu.VMEM((2, 512, 256), BF16),
            pltpu.VMEM((2, 512, 256), BF16),
            pltpu.VMEM((512, 128), F32),
            pltpu.VMEM((64, 128), F32),
            pltpu.VMEM((4, 6, 64, 256), BF16),
            pltpu.VMEM((3, 4, 32, 256), BF16),
            pltpu.VMEM((6, 3, 16, 256), BF16),
            pltpu.VMEM((16, 256), BF16),
            pltpu.VMEM((49, 7, 32, 128), BF16),
            pltpu.VMEM((3, 3, 7, 128, 128), BF16),
            pltpu.VMEM((2, 2, 192, 256), BF16),
            pltpu.VMEM((2, 256, 256), BF16),
            pltpu.VMEM((592, 256), F32),
            pltpu.VMEM((10, 2, 128, 128), F32),
            pltpu.VMEM((128, 512), F32),
            pltpu.SemaphoreType.DMA,
            pltpu.SemaphoreType.DMA((len(RUNS),)),
            pltpu.SemaphoreType.DMA((8,)),
            pltpu.SemaphoreType.DMA((8,)),
            pltpu.SemaphoreType.DMA((8,)),
            pltpu.SemaphoreType.DMA((8,)),
            pltpu.SemaphoreType.DMA((17,)),
            pltpu.SemaphoreType.DMA((6, 3)),
        ],
        compiler_params=pltpu.CompilerParams(
            collective_id=0, has_side_effects=True, vmem_limit_bytes=48 * 1024 * 1024
        ),
        name="far_field",
    )(leaf_multipoles.reshape(2048, 128), m2l_ops, proj_in, proj_out, m2m)
    return made.reshape(leaf_multipoles.shape)


def solution(mesh):
    placed = (P(None, "gx", "gy", None), P(), P(), P(), P())
    return jax.shard_map(
        functools.partial(per_device, n_gx=mesh.shape["gx"], n_gy=mesh.shape["gy"]),
        mesh=mesh,
        in_specs=placed,
        out_specs=P(None, "gx", "gy", None),
        check_vma=False,
    )
```

profile of v0, /device:TPU:1, one launch (start us, length us, event | category | flops | bytes accessed | tf_op | source)
XLA Modules:
  0.0 36.2 jit_solution(8720234490255616753)
XLA Ops:
  0.0 0.0 copy-start.1
  0.0 0.0 copy-start.2
  0.0 0.8 %copy.7.pout_ref = f32[64,32]{1,0:T(8,128)S(1)} copy(f32[64,32]{0,1:T(8,128)} %param.8) | data formatting | bytes 16384 | tf_op args[3]
  0.8 5.7 %copy.6.ops_hbm = bf16[316,32,32]{2,1,0:T(8,128)(2,1)S(1)} copy(bf16[316,32,32]{0,2,1:T(8,128)(2,1)} %param.6) | data formatting | bytes 1294336 | tf_op args[1]
  6.5 0.0 copy-done.1
  6.6 0.0 copy-done.2
  6.6 0.0 copy-start
  6.6 1.2 %copy-done = f32[64,4,8,128]{3,2,1,0:T(8,128)S(1)} copy-done((f32[64,4,8,128]{3,2,1,0:T(8,128)S(1)}, f32[64,4,8,128]{3,2,1,0:T(8,128)}, u32[]{:S(2)}) %copy-start) | copy-done | bytes 1048600
  7.8 27.4 %far_field.1 = f32[2048,128]{1,0:T(8,128)S(1)} custom-call(f32[2048,128]{1,0:T(8,128)S(1)} %bitcast.3, bf16[316,32,32]{2,1,0:T(8,128)(2,1)S(1)} %copy.6.ops_hbm, f32[32,64]{1,0:T(8,128)S(1)} %copy-done.2, f32[64,32]{1,0:T(8,128)S(1)} %copy.7.pout_ref, f32[8,64,64]{2,1,0:T(8,128)S(1)} %copy-done.1), custom_call_target="tpu_custom_call" | custom-call | tf_op jit(solution)/shard_map/far_field/pallas_call | solution.py:348
  35.2 1.0 %copy.9 = f32[64,4,8,128]{3,2,1,0:T(8,128)} copy(f32[64,4,8,128]{3,2,1,0:T(8,128)S(1)} %bitcast.2) | data formatting | bytes 2097152
Async XLA Ops:
  0.0 6.6 %copy-start.1 = (f32[8,64,64]{2,1,0:T(8,128)S(1)}, f32[8,64,64]{2,1,0:T(8,128)}, u32[]{:S(2)}) copy-start(f32[8,64,64]{2,1,0:T(8,128)} %m2m_ref.1) | copy-start | bytes 393220
  0.0 6.6 %copy-start.2 = (f32[32,64]{1,0:T(8,128)S(1)}, f32[32,64]{1,0:T(8,128)}, u32[]{:S(2)}) copy-start(f32[32,64]{1,0:T(8,128)} %pin_ref.1) | copy-start | bytes 24580
  6.6 1.2 %copy-start = (f32[64,4,8,128]{3,2,1,0:T(8,128)S(1)}, f32[64,4,8,128]{3,2,1,0:T(8,128)}, u32[]{:S(2)}) copy-start(f32[64,4,8,128]{3,2,1,0:T(8,128)} %param.5) | copy-start | bytes 3145732
where the time goes:
time: 36.3 us; the launch traced here: 36.2 us
  Pallas kernels  27.4 us (75%)
  local copies, waits for them, and re-layouts  8.74 us (24%)
    pallas_call x1, Pallas kernels, per_device(): pl.pallas_call(functools.partial(kernel, n_gx, n_gy), out_shape=jax.Shape...  27.4 us
    unnamed x9, local copies, waits for them, and re-layouts  8.74 us

commit v1 on v0

--- a/solution.py
+++ b/solution.py
@@ -34,24 +34,6 @@
     return lax.broadcasted_iota(jnp.int32, shape, 0)
 
 
-def hole_runs():
-    runs, first, number = [], 0, 0
-    position = 0
-    for ox in range(-3, 4):
-        for oy in range(-3, 4):
-            for oz in range(-3, 4):
-                near = max(abs(ox), abs(oy), abs(oz)) < 2
-                if not near:
-                    if runs and runs[-1][0] + runs[-1][2] == position:
-                        runs[-1][2] += 1
-                    else:
-                        runs.append([position, number, 1])
-                    number += 1
-                position += 1
-    return runs
-
-
-RUNS = hole_runs()
 NEIGHBOURS = [(1, 0), (-1, 0), (0, 1), (0, -1), (1, 1), (1, -1), (-1, 1), (-1, -1)]
 
 
@@ -59,7 +41,7 @@
     n_gx, n_gy,
     x_hbm, ops_hbm, pin_ref, pout_ref, m2m_ref,
     out_ref,
-    x_ref, ops_ref, turn_ref, dh_ref, dl_ref, m1_ref, m2_ref, src0, src1, cin, cout, rep_ref, q_ref,
+    x_ref, ops_ref, wide_ref, turn_ref, dh_ref, dl_ref, m1_ref, m2_ref, src0, src1, cin, cout, rep_ref, q_ref,
     wup_ref, wd_ref, far_ref, h_ref, l1_ref,
     in_sem, ops_sem, send0, recv0, send1, recv1, send2, recv2,
 ):
@@ -75,22 +57,45 @@
     ]
     coarse_moves = [(far_dx if dx is None else dx, dy) for dx, dy in coarse_moves]
 
-    barrier = pltpu.get_barrier_semaphore()
-    for dx, dy in coarse_moves:
-        pl.semaphore_signal(barrier, inc=1, device_id=device(dx, dy), device_id_type=MESH)
+    def exists(dx, dy):
+        x, y = px + dx, py + dy
+        return (x >= 0) & (x < n_gx) & (y >= 0) & (y < n_gy)
 
     x_copy = pltpu.make_async_copy(x_hbm, x_ref, in_sem)
     x_copy.start()
-    ops_copies = []
-    for k, (position, number, count) in enumerate(RUNS):
-        copy = pltpu.make_async_copy(
-            ops_hbm.at[pl.ds(number, count)], ops_ref.at[pl.ds(position, count)], ops_sem.at[k]
-        )
-        copy.start()
-        ops_copies.append(copy)
-    for ox in (2, 3, 4):
-        for oy in (2, 3, 4):
-            ops_ref[pl.ds((ox * 7 + oy) * 7 + 2, 3)] = jnp.zeros((3, 32, 32), BF16)
+    ops_copy = pltpu.make_async_copy(ops_hbm, ops_ref, ops_sem)
+    ops_copy.start()
+
+    cin[...] = jnp.zeros(cin.shape, BF16)
+
+    @pl.when(px == 0)
+    def _():
+        src0[0] = jnp.zeros(src0.shape[1:], BF16)
+        src1[0] = jnp.zeros(src1.shape[1:], BF16)
+
+    @pl.when(px == n_gx - 1)
+    def _():
+        src0[3] = jnp.zeros(src0.shape[1:], BF16)
+        src1[2] = jnp.zeros(src1.shape[1:], BF16)
+
+    @pl.when(py == 0)
+    def _():
+        src0[:, 0] = jnp.zeros((4, 64, 256), BF16)
+        src1[:, 0] = jnp.zeros((3, 32, 256), BF16)
+
+    @pl.when(py == n_gy - 1)
+    def _():
+        src0[:, 5] = jnp.zeros((4, 64, 256), BF16)
+        src1[:, 3] = jnp.zeros((3, 32, 256), BF16)
+
+    barrier = pltpu.get_barrier_semaphore()
+    greeted = 0
+    for dx, dy in coarse_moves:
+        greeted = greeted + exists(dx, dy).astype(jnp.int32)
+
+        @pl.when(exists(dx, dy))
+        def _():
+            pl.semaphore_signal(barrier, inc=1, device_id=device(dx, dy), device_id_type=MESH)
 
     pin = pin_ref[...]
     pin2 = jnp.concatenate([pin, pin], axis=1)
@@ -102,7 +107,7 @@
         high, low = split(jnp.concatenate([pack, mix], axis=0))
         wup_ref[sz, 0] = high
         wup_ref[sz, 1] = low
-    pout = pout_ref[...]
+    pout = pout_ref[...].T
     pout2 = jnp.concatenate([pout, pout], axis=1)
     pout4 = jnp.concatenate([pout2, pout2], axis=1)
     unpack = jnp.concatenate([pout4, pout4, pout4, pout4], axis=0)
@@ -173,7 +178,7 @@
         made = dot3(high, low, wup_ref[sz, 0, 0:128], wup_ref[sz, 1, 0:128])
         cout[:, sz * 128 : (sz + 1) * 128] = made.astype(BF16)
 
-    pl.semaphore_wait(barrier, len(coarse_moves))
+    pl.semaphore_wait(barrier, greeted)
 
     copies = []
     for k, (dx, dy) in enumerate(NEIGHBOURS):
@@ -190,8 +195,8 @@
                 device_id=device(dx, dy),
                 device_id_type=MESH,
             )
-            copy.start()
-            copies.append(copy)
+            pl.when(exists(dx, dy))(copy.start)
+            copies.append((copy, dx, dy))
     coarse_copies = []
     for k, (dx, dy) in enumerate(coarse_moves):
         to_parity = lax.rem(px + (dx + n_gx), 2)
@@ -204,21 +209,34 @@
             device_id=device(dx, dy),
             device_id_type=MESH,
         )
-        copy.start()
+        pl.when(exists(dx, dy))(copy.start)
         coarse_copies.append(copy)
     cin[2 + parity, 1] = cout[...]
 
-    for copy in ops_copies:
-        copy.wait()
-    spread = jnp.where(lanes((32, 128)) % 32 == rows((32, 128)), 1.0, 0.0).astype(BF16)
+    position, number = rows((344, 316)), lanes((344, 316))
+    ox, oy, oz = position // 49, position // 7 % 7, position % 7
+    in_x, in_y, in_z = (abs(ox - 3) < 2, abs(oy - 3) < 2, abs(oz - 3) < 2)
+    before = jnp.clip(ox - 2, 0, 3) * 9
+    before = before + jnp.where(in_x, jnp.clip(oy - 2, 0, 3) * 3, 0)
+    before = before + jnp.where(in_x & in_y, jnp.clip(oz - 2, 0, 3), 0)
+    wanted = jnp.where(in_x & in_y & in_z, -1, position - before)
+    pick = jnp.where(wanted == number, 1.0, 0.0).astype(BF16)
+    ops_copy.wait()
 
     def replicate(k, _):
-        blocks = ops_ref[pl.ds(k * 7, 7)].reshape(224, 32)
-        made = jnp.dot(blocks, spread, preferred_element_type=F32).astype(BF16)
-        rep_ref[k] = made.reshape(7, 32, 128)
+        one, two = ops_ref[2 * k], ops_ref[2 * k + 1]
+        made = dot_nt(pick, jnp.concatenate([one, one, one, one, two, two, two, two], axis=0))
+        wide_ref[pl.ds(2 * k, 344, stride=32), :] = made[:, :128]
+        wide_ref[pl.ds(2 * k + 1, 344, stride=32), :] = made[:, 128:]
         return 0
 
-    lax.fori_loop(0, 49, replicate, 0)
+    lax.fori_loop(0, 16, replicate, 0)
+
+    def narrow(k, _):
+        rep_ref[k] = wide_ref[pl.ds(k * 224, 224), :].astype(BF16).reshape(7, 32, 128)
+        return 0
+
+    lax.fori_loop(0, 49, narrow, 0)
     place = lanes((224, 128)) // 32
 
     def assemble(k, _):
@@ -236,39 +254,21 @@
 
     lax.fori_loop(0, 9, assemble, 0)
 
-    for copy in copies:
-        copy.wait()
+    for copy, dx, dy in copies:
+        pl.when(exists(dx, dy))(copy.wait_send)
+        pl.when(exists(-dx, -dy))(copy.wait_recv)
     for k, (dx, dy) in enumerate(coarse_moves):
-        coarse_copies[k].wait_send()
         slot = dx + 2 + parity
-        pltpu.make_async_remote_copy(
+        arrival = pltpu.make_async_remote_copy(
             src_ref=cout,
             dst_ref=cin.at[slot, 1 + dy],
             send_sem=send2.at[k],
             recv_sem=recv2.at[slot, 1 + dy],
             device_id=device(dx, dy),
             device_id_type=MESH,
-        ).wait_recv()
-
-    @pl.when(px == 0)
-    def _():
-        src0[0] = jnp.zeros(src0.shape[1:], BF16)
-        src1[0] = jnp.zeros(src1.shape[1:], BF16)
-
-    @pl.when(px == n_gx - 1)
-    def _():
-        src0[3] = jnp.zeros(src0.shape[1:], BF16)
-        src1[2] = jnp.zeros(src1.shape[1:], BF16)
-
-    @pl.when(py == 0)
-    def _():
-        src0[:, 0] = jnp.zeros((4, 64, 256), BF16)
-        src1[:, 0] = jnp.zeros((3, 32, 256), BF16)
-
-    @pl.when(py == n_gy - 1)
-    def _():
-        src0[:, 5] = jnp.zeros((4, 64, 256), BF16)
-        src1[:, 3] = jnp.zeros((3, 32, 256), BF16)
+        )
+        pl.when(exists(dx, dy))(coarse_copies[k].wait_send)
+        pl.when(exists(dx, dy))(arrival.wait_recv)
 
     acc = None
     sums = []
@@ -276,10 +276,7 @@
         acc = None
         for mx in range(3):
             for my in range(3):
-                parent_x, parent_y = px // 2 + mx - 1, py + my - 1
-                inside = (parent_x >= 0) & (parent_x < n_gx // 2) & (parent_y >= 0) & (parent_y < n_gy)
                 coarse = cin[2 * mx, my] + cin[2 * mx + 1, my]
-                coarse = jnp.where(inside, coarse, jnp.zeros_like(coarse))
                 source = jnp.concatenate(
                     [
                         src0[mx : mx + 2, my : my + 4].reshape(512, 256),
@@ -344,7 +341,7 @@
 
 def per_device(leaf_multipoles, m2l_ops, proj_in, proj_out, m2m, n_gx, n_gy):
     vmem = pl.BlockSpec(memory_space=pltpu.VMEM)
-    hbm = pl.BlockSpec(memory_space=pl.ANY)
+    hbm = pl.BlockSpec(memory_space=pltpu.HBM)
     made = pl.pallas_call(
         functools.partial(kernel, n_gx, n_gy),
         out_shape=jax.ShapeDtypeStruct((2048, 128), F32),
@@ -352,7 +349,8 @@
         out_specs=vmem,
         scratch_shapes=[
             pltpu.VMEM((2048, 128), F32),
-            pltpu.VMEM((343, 32, 32), BF16),
+            pltpu.VMEM((32, 32, 316), BF16),
+            pltpu.VMEM((344 * 32, 128), F32),
             pltpu.VMEM((8, 2, 128, 128), F32),
             pltpu.VMEM((2, 512, 256), BF16),
             pltpu.VMEM((2, 512, 256), BF16),
@@ -370,7 +368,7 @@
             pltpu.VMEM((10, 2, 128, 128), F32),
             pltpu.VMEM((128, 512), F32),
             pltpu.SemaphoreType.DMA,
-            pltpu.SemaphoreType.DMA((len(RUNS),)),
+            pltpu.SemaphoreType.DMA,
             pltpu.SemaphoreType.DMA((8,)),
             pltpu.SemaphoreType.DMA((8,)),
             pltpu.SemaphoreType.DMA((8,)),
@@ -382,7 +380,7 @@
             collective_id=0, has_side_effects=True, vmem_limit_bytes=48 * 1024 * 1024
         ),
         name="far_field",
-    )(leaf_multipoles.reshape(2048, 128), m2l_ops, proj_in, proj_out, m2m)
+    )(leaf_multipoles.reshape(2048, 128), m2l_ops.transpose(1, 2, 0), proj_in, proj_out.T, m2m)
     return made.reshape(leaf_multipoles.shape)
 
 

time: 36.3 us -> 28.2 us (0.78)
  the two profiles are of different devices: /device:TPU:1 before, /device:TPU:109 now
where the time goes in v1:
time: 28.2 us; the launch traced here: 27.9 us
  Pallas kernels  22.2 us (79%)
  local copies, waits for them, and re-layouts  5.71 us (20%)
    pallas_call x1, Pallas kernels, per_device(): pl.pallas_call(functools.partial(kernel, n_gx, n_gy), out_shape=jax.Shape...  22.2 us
    unnamed x11, local copies, waits for them, and re-layouts  5.71 us

profile of v1, /device:TPU:109, one launch (start us, length us, event | category | flops | bytes accessed | tf_op | source)
XLA Modules:
  0.0 27.9 jit_solution(14023123173543180150)
XLA Ops:
  0.0 0.0 copy-start
  0.0 1.2 %copy-done = f32[64,4,8,128]{3,2,1,0:T(8,128)S(1)} copy-done((f32[64,4,8,128]{3,2,1,0:T(8,128)S(1)}, f32[64,4,8,128]{3,2,1,0:T(8,128)}, u32[]{:S(2)}) %copy-start) | copy-done | bytes 1048600
  1.2 0.0 copy-start.1
  1.2 1.1 %copy-done.1 = bf16[316,32,32]{0,2,1:T(8,128)(2,1)S(1)} copy-done((bf16[316,32,32]{0,2,1:T(8,128)(2,1)S(1)}, bf16[316,32,32]{0,2,1:T(8,128)(2,1)}, u32[]{:S(2)}) %copy-start.1) | copy-done | bytes 647192
  2.4 0.0 copy-start.2
  2.4 0.9 %copy-done.2 = f32[8,64,64]{2,1,0:T(8,128)S(1)} copy-done((f32[8,64,64]{2,1,0:T(8,128)S(1)}, f32[8,64,64]{2,1,0:T(8,128)}, u32[]{:S(2)}) %copy-start.2) | copy-done | bytes 131096
  3.3 0.0 copy-start.3
  3.3 0.7 %copy-done.3 = f32[32,64]{1,0:T(8,128)S(1)} copy-done((f32[32,64]{1,0:T(8,128)S(1)}, f32[32,64]{1,0:T(8,128)}, u32[]{:S(2)}) %copy-start.3) | copy-done | bytes 8216
  4.0 0.0 copy-start.4
  4.0 0.7 %copy-done.4 = f32[64,32]{0,1:T(8,128)S(1)} copy-done((f32[64,32]{0,1:T(8,128)S(1)}, f32[64,32]{0,1:T(8,128)}, u32[]{:S(2)}) %copy-start.4) | copy-done | bytes 8216
  4.7 22.2 %far_field.1 = f32[2048,128]{1,0:T(8,128)S(1)} custom-call(f32[2048,128]{1,0:T(8,128)S(1)} %bitcast.5, bf16[32,32,316]{2,1,0:T(8,128)(2,1)S(1)} %bitcast.6, f32[32,64]{1,0:T(8,128)S(1)} %copy-done.3, f32[32,64]{1,0:T(8,128)S(1)} %bitcast.7, f32[8,64,64]{2,1,0:T(8,128)S(1)} %copy-done.2), custom_call_target="tpu_custom_call" | custom-call | tf_op jit(solution)/shard_map/far_field/pallas_call | solution.py:345
  27.0 1.0 %copy.7 = f32[64,4,8,128]{3,2,1,0:T(8,128)} copy(f32[64,4,8,128]{3,2,1,0:T(8,128)S(1)} %bitcast.4) | data formatting | bytes 2097152
Async XLA Ops:
  0.0 1.2 %copy-start = (f32[64,4,8,128]{3,2,1,0:T(8,128)S(1)}, f32[64,4,8,128]{3,2,1,0:T(8,128)}, u32[]{:S(2)}) copy-start(f32[64,4,8,128]{3,2,1,0:T(8,128)} %param.5) | copy-start | bytes 3145732
  1.2 1.1 %copy-start.1 = (bf16[316,32,32]{0,2,1:T(8,128)(2,1)S(1)}, bf16[316,32,32]{0,2,1:T(8,128)(2,1)}, u32[]{:S(2)}) copy-start(bf16[316,32,32]{0,2,1:T(8,128)(2,1)} %param.6) | copy-start | bytes 1941508
  2.4 0.9 %copy-start.2 = (f32[8,64,64]{2,1,0:T(8,128)S(1)}, f32[8,64,64]{2,1,0:T(8,128)}, u32[]{:S(2)}) copy-start(f32[8,64,64]{2,1,0:T(8,128)} %m2m_ref.1) | copy-start | bytes 393220
  3.3 0.7 %copy-start.3 = (f32[32,64]{1,0:T(8,128)S(1)}, f32[32,64]{1,0:T(8,128)}, u32[]{:S(2)}) copy-start(f32[32,64]{1,0:T(8,128)} %pin_ref.1) | copy-start | bytes 24580
  4.0 0.7 %copy-start.4 = (f32[64,32]{0,1:T(8,128)S(1)}, f32[64,32]{0,1:T(8,128)}, u32[]{:S(2)}) copy-start(f32[64,32]{0,1:T(8,128)} %param.8) | copy-start | bytes 24580

commit v2 on v1

v2 whole, which is shorter than its diff:
```python
import functools

import jax
import jax.numpy as jnp
from jax import lax
from jax.experimental import pallas as pl
from jax.experimental.pallas import tpu as pltpu
from jax.sharding import PartitionSpec as P

MESH = pl.DeviceIdType.MESH
F32 = jnp.float32
BF16 = jnp.bfloat16
NT = (((1,), (1,)), ((), ()))


def dot_nt(a, b):
    return lax.dot_general(a, b, NT, preferred_element_type=F32)


def split(value):
    high = value.astype(BF16)
    return high, (value - high.astype(F32)).astype(BF16)


def dot3(a_high, a_low, b_high, b_low):
    return dot_nt(a_high, b_high) + (dot_nt(a_low, b_high) + dot_nt(a_high, b_low))


def lanes(shape):
    return lax.broadcasted_iota(jnp.int32, shape, 1)


def rows(shape):
    return lax.broadcasted_iota(jnp.int32, shape, 0)


MESSAGES = 27


def kernel(
    n_gx, n_gy,
    x_hbm, ops_hbm, pin_hbm, pout_hbm, m2m_hbm,
    out_ref,
    pin_ref, pout_ref, m2m_ref, x_ref, ops_ref, wide_ref, turn_ref, dh_ref, dl_ref, m1_ref, m2_ref, src0, src1, cin, q_ref,
    wup_ref, wd_ref, acc_ref, far_ref, h_ref, l1_ref,
    in_sem, ops_sem, weight_sem, sent, came, coarse_came,
):
    px, py = lax.axis_index("gx"), lax.axis_index("gy")
    parity = lax.rem(px, 2)
    far_dx = 3 - 6 * parity

    def device(dx, dy):
        return (lax.rem(px + (dx + n_gx), n_gx), lax.rem(py + (dy + n_gy), n_gy))

    def exists(dx, dy):
        x, y = px + dx, py + dy
        return (x >= 0) & (x < n_gx) & (y >= 0) & (y < n_gy)

    weight_copies = [
        pltpu.make_async_copy(source, target, weight_sem.at[k])
        for k, (source, target) in enumerate(((pin_hbm, pin_ref), (m2m_hbm, m2m_ref), (pout_hbm, pout_ref)))
    ]
    for copy in weight_copies:
        copy.start()
    x_copies = [
        pltpu.make_async_copy(x_hbm.at[:, pl.ds(16 * X, 16)], x_ref.at[X], in_sem.at[X]) for X in range(2)
    ]
    for copy in x_copies:
        copy.start()
    ops_copy = pltpu.make_async_copy(ops_hbm, ops_ref, ops_sem)
    ops_copy.start()

    cin[...] = jnp.zeros(cin.shape, BF16)

    @pl.when(px == 0)
    def _():
        src0[0] = jnp.zeros(src0.shape[1:], BF16)
        src1[0] = jnp.zeros(src1.shape[1:], BF16)

    @pl.when(px == n_gx - 1)
    def _():
        src0[3] = jnp.zeros(src0.shape[1:], BF16)
        src1[2] = jnp.zeros(src1.shape[1:], BF16)

    @pl.when(py == 0)
    def _():
        src0[:, 0] = jnp.zeros((4, 64, 256), BF16)
        src1[:, 0] = jnp.zeros((3, 32, 256), BF16)
        cin[0] = jnp.zeros(cin.shape[1:], BF16)

    @pl.when(py == n_gy - 1)
    def _():
        src0[:, 5] = jnp.zeros((4, 64, 256), BF16)
        src1[:, 3] = jnp.zeros((3, 32, 256), BF16)
        cin[2] = jnp.zeros(cin.shape[1:], BF16)

    barrier = pltpu.get_barrier_semaphore()
    greeted = 0
    for dx, dy in ((1, 0), (-1, 0), (0, 1), (0, -1), (2, 0), (-2, 0), (far_dx, 0)):
        greeted = greeted + exists(dx, dy).astype(jnp.int32)

        @pl.when(exists(dx, dy))
        def _():
            pl.semaphore_signal(barrier, inc=1, device_id=device(dx, dy), device_id_type=MESH)

    used = []
    waits = []

    def message(source, target, dx, dy, column=None, came_sem=None):
        k = len(used)
        used.append(k)
        copy = pltpu.make_async_remote_copy(
            src_ref=source,
            dst_ref=target,
            send_sem=sent.at[k],
            recv_sem=came.at[k] if came_sem is None else came_sem,
            device_id=device(dx, dy),
            device_id_type=MESH,
        )
        going, coming = exists(dx, dy), exists(-dx, -dy)
        if column is not None:
            going, coming = going & exists(column, 0), coming & exists(column, 0)
        waits.append((going, copy))
        return copy, going, coming

    def start(item):
        pl.when(item[1])(item[0].start)

    def arrive(item):
        pl.when(item[2])(item[0].wait_recv)

    SIDES = (1, -1)
    near = {1: 0, -1: 1}
    leaf_x, leaf_y, leaf_xy, mid_x, mid_y, mid_xy, coarse_y = {}, {}, {}, {}, {}, {}, {}
    for dx in SIDES:
        column, halo = (2, 0) if dx == 1 else (1, 3)
        for first, count in ((4, 1), (1, 1), (2, 2)):
            part = pl.ds(first, count)
            leaf_x[dx, first] = message(src0.at[column, part], src0.at[halo, part], dx, 0)
        mid_x[dx] = message(src1.at[1, pl.ds(1, 2)], src1.at[1 - dx, pl.ds(1, 2)], dx, 0)
    for dy in SIDES:
        row, halo = (4, 0) if dy == 1 else (1, 5)
        row1, halo1 = (2, 0) if dy == 1 else (1, 3)
        leaf_y[dy] = message(src0.at[pl.ds(1, 2), row], src0.at[pl.ds(1, 2), halo], 0, dy)
        mid_y[dy] = message(src1.at[1, row1], src1.at[1, halo1], 0, dy)
        coarse_y[dy] = message(cin.at[1], cin.at[1 - dy], 0, dy)
        for dx in SIDES:
            column = 0 if dx == 1 else 3
            leaf_xy[dx, dy] = message(src0.at[column, row], src0.at[column, halo], 0, dy, -dx)
            mid_xy[dx, dy] = message(src1.at[1 - dx, row1], src1.at[1 - dx, halo1], 0, dy, -dx)
    coarse_x = []
    own = cin.at[1, 2 + parity]
    for dx in (far_dx, 2, -2, 1, -1):
        slot = (2 - dx) + lax.rem(px + (dx + n_gx), 2)
        coarse_x.append(message(own, cin.at[1, slot], dx, 0, came_sem=coarse_came.at[slot]))
    coarse_arrivals = []
    for k, dx in enumerate((far_dx, 2, -2, 1, -1)):
        slot = dx + 2 + parity
        copy = pltpu.make_async_remote_copy(
            src_ref=own,
            dst_ref=cin.at[1, slot],
            send_sem=sent.at[0],
            recv_sem=coarse_came.at[slot],
            device_id=device(dx, 0),
            device_id_type=MESH,
        )
        coarse_arrivals.append((copy, None, exists(dx, 0)))

    for copy in weight_copies:
        copy.wait()
    pin = pin_ref[...]
    pin2 = jnp.concatenate([pin, pin], axis=1)
    pin4 = jnp.concatenate([pin2, pin2], axis=1)
    pack = jnp.concatenate([pin4, pin4, pin4, pin4], axis=0)
    pack = jnp.where(rows(pack.shape) // 32 == lanes(pack.shape) // 64, pack, 0.0)
    for sz in range(2):
        mix = jnp.concatenate([m2m_ref[2 * s + sz] for s in range(4)], axis=1)
        high, low = split(jnp.concatenate([pack, mix], axis=0))
        wup_ref[sz, 0] = high
        wup_ref[sz, 1] = low

    flat_ref = x_ref.reshape(2048, 128)
    for X in range(2):
        x_copies[X].wait()
        for Y in range(4):
            parent = X * 4 + Y
            block = jnp.concatenate(
                [
                    flat_ref[pl.ds(X * 1024 + sx * 8 + 2 * Y + sy, 64, stride=16), :]
                    for sx in range(2)
                    for sy in range(2)
                ],
                axis=0,
            )
            turned = block.T
            turn_ref[parent, 0] = turned[:, :128]
            turn_ref[parent, 1] = turned[:, 128:]
            for sz in range(2):
                high, low = split(
                    jnp.concatenate(
                        [turn_ref[parent, sx, pl.ds(sz, 64, stride=2), :] for sx in range(2)], axis=1
                    )
                )
                dh_ref[sz, pl.ds(parent * 64, 64)] = high
                dl_ref[sz, pl.ds(parent * 64, 64)] = low
    total = None
    for sz in range(2):
        made = dot3(dh_ref[sz], dl_ref[sz], wup_ref[sz, 0], wup_ref[sz, 1])
        src0[1:3, 1:5, :, sz * 128 : (sz + 1) * 128] = made[:, :128].astype(BF16).reshape(2, 4, 64, 128)
        total = made[:, 128:] if sz == 0 else total + made[:, 128:]
    m1_ref[:, 0:64] = total
    pl.semaphore_wait(barrier, greeted)
    for first in (4, 1, 2):
        for dx in SIDES:
            start(leaf_x[dx, first])
    for dy in SIDES:
        start(leaf_y[dy])

    total = None
    for sz in range(2):
        block = jnp.concatenate(
            [
                jnp.concatenate(
                    [
                        m1_ref[pl.ds((sx * 4 + 2 * Y1 + sy) * 64 + sz, 32, stride=2), :][:, 0:64]
                        for sx in range(2)
                        for sy in range(2)
                    ],
                    axis=1,
                )
                for Y1 in range(2)
            ],
            axis=0,
        )
        high, low = split(block)
        made = dot3(high, low, wup_ref[sz, 0], wup_ref[sz, 1])
        src1[1, 1:3, :, sz * 128 : (sz + 1) * 128] = made[:, :128].astype(BF16).reshape(2, 32, 128)
        total = made[:, 128:] if sz == 0 else total + made[:, 128:]
    m2_ref[:, 0:64] = total
    for dx in SIDES:
        start(mid_x[dx])
    for dy in SIDES:
        start(mid_y[dy])

    pieces = []
    for sz in range(2):
        pair = jnp.concatenate(
            [m2_ref[pl.ds(sy * 32 + sz, 16, stride=2), :][:, 0:64] for sy in range(2)], axis=1
        )
        high, low = split(pair)
        pieces.append(dot3(high, low, wup_ref[0, 0, 0:64, 0:128], wup_ref[0, 1, 0:64, 0:128]))
    cin[1, 2 + parity] = jnp.concatenate(pieces, axis=1).astype(BF16)
    for item in coarse_x:
        start(item)

    position, number = rows((344, 316)), lanes((344, 316))
    ox, oy, oz = position // 49, position // 7 % 7, position % 7
    in_x, in_y, in_z = (abs(ox - 3) < 2, abs(oy - 3) < 2, abs(oz - 3) < 2)
    before = jnp.clip(ox - 2, 0, 3) * 9
    before = before + jnp.where(in_x, jnp.clip(oy - 2, 0, 3) * 3, 0)
    before = before + jnp.where(in_x & in_y, jnp.clip(oz - 2, 0, 3), 0)
    wanted = jnp.where(in_x & in_y & in_z, -1, position - before)
    pick = jnp.where(wanted == number, 1.0, 0.0).astype(BF16)
    ops_copy.wait()
    for pair in range(4):
        slab = jnp.concatenate([ops_ref[2 * pair + g + 8 * four] for g in range(2) for four in range(4)], axis=0)
        made = dot_nt(pick, slab)
        wide_ref[pair * 688 : pair * 688 + 344, :] = made[:, :128]
        wide_ref[pair * 688 + 344 : pair * 688 + 688, :] = made[:, 128:]

    for first in (4, 1):
        for dx in SIDES:
            arrive(leaf_x[dx, first])
            start(leaf_xy[dx, 1 if first == 4 else -1])
    for dx in SIDES:
        arrive(mid_x[dx])
        for dy in SIDES:
            start(mid_xy[dx, dy])
    for item in coarse_arrivals:
        arrive(item)
    for dy in SIDES:
        start(coarse_y[dy])

    place = lanes((8, 128)) // 32

    def assemble(k, _):
        mx, my = k // 3, k % 3
        for tx in range(2):
            for ty in range(2):
                for oz in range(7):
                    tiles = []
                    for sx in range(2):
                        for sy in range(2):
                            p = ((2 * mx + 1 + sx - tx) * 7 + 2 * my + 1 + sy - ty) * 7 + oz
                            tiles.append(wide_ref[pl.ds(p, 8, stride=344), :])
                    turned = []
                    for r in range(4):
                        made = tiles[r]
                        for q in range(1, 4):
                            made = jnp.where(place == q, tiles[(q + r) % 4], made)
                        turned.append(made if r == 0 else pltpu.roll(made, 32 * r, 1))
                    made = []
                    for four in range(4):
                        piece = turned[-four % 4]
                        for q in range(1, 4):
                            piece = jnp.where(place == q, turned[(q - four) % 4], piece)
                        made.append(piece)
                    q_ref[mx, my, oz, (2 * tx + ty) * 32 : (2 * tx + ty) * 32 + 32] = jnp.concatenate(
                        made, axis=0
                    ).astype(BF16)
        return 0

    lax.fori_loop(0, 9, assemble, 0)

    def weight(mx, my, mz):
        return jnp.concatenate(
            [
                q_ref[mx, my, 2 * mz : 2 * mz + 2].reshape(256, 128),
                q_ref[mx, my, 2 * mz + 1 : 2 * mz + 3].reshape(256, 128),
            ],
            axis=1,
        )

    def shifted(sums, size):
        inner = rows(sums[0].shape) & (size - 1)
        count = sums[0].shape[0]
        below = jnp.where(inner == 0, 0.0, pltpu.roll(sums[0], 1, 0))
        above = jnp.where(inner == size - 1, 0.0, pltpu.roll(sums[2], count - 1, 0))
        return sums[1] + below + above

    for dy in SIDES:
        arrive(leaf_y[dy])
    for mz in range(3):
        acc = None
        for my in range(3):
            both = dot_nt(src0[1:3, my : my + 4].reshape(512, 256), weight(1, my, mz))
            lower = dot_nt(src0[2, my : my + 4].reshape(256, 256), weight(2, my, mz))
            upper = dot_nt(src0[1, my : my + 4].reshape(256, 256), weight(0, my, mz))
            made = both + jnp.concatenate([lower, upper], axis=0)
            acc = made if acc is None else acc + made
        acc_ref[mz] = acc

    for dy in SIDES:
        arrive(mid_y[dy])
        arrive(coarse_y[dy])
        for dx in SIDES:
            arrive(mid_xy[dx, dy])
    sums = []
    for mz in range(3):
        acc = None
        for mx in range(3):
            for my in range(3):
                one, two = cin[my, 2 * mx], cin[my, 2 * mx + 1]
                coarse = jnp.concatenate([one[:, :64], two[:, :64], one[:, 64:], two[:, 64:]], axis=1)
                source = jnp.concatenate([src1[mx, my : my + 2].reshape(64, 256), coarse], axis=0)
                made = dot_nt(source, weight(mx, my, mz))
                acc = made if acc is None else acc + made
        sums.append(acc)
    far1 = shifted([acc[0:64] for acc in sums], 32)
    far2 = shifted([acc[64:80] for acc in sums], 16)

    pout = pout_ref[...].T
    pout2 = jnp.concatenate([pout, pout], axis=1)
    pout4 = jnp.concatenate([pout2, pout2], axis=1)
    unpack = jnp.concatenate([pout4, pout4, pout4, pout4], axis=0)
    unpack = jnp.where(rows(unpack.shape) // 64 == lanes(unpack.shape) // 32, unpack, 0.0)
    down = jnp.concatenate([m2m_ref[2 * s : 2 * s + 2].reshape(128, 64).T for s in range(4)], axis=0)
    high, low = split(jnp.concatenate([unpack, down], axis=1))
    wd_ref[0] = high
    wd_ref[1] = low
    wd_high, wd_low = wd_ref[0], wd_ref[1]
    twice_high = jnp.concatenate([wd_high[k * 64 : k * 64 + 64] for k in (0, 0, 1, 1, 2, 2, 3, 3)], axis=0)
    twice_low = jnp.concatenate([wd_low[k * 64 : k * 64 + 64] for k in (0, 0, 1, 1, 2, 2, 3, 3)], axis=0)

    for tz in range(2):
        part = slice(128, 256) if tz == 0 else slice(0, 128)
        h_ref[0, 0, pl.ds(tz, 16, stride=2), :] = far2[:, part] * 0.25
        for Y1 in range(2):
            h_ref[1, 0, pl.ds(Y1 * 64 + tz, 32, stride=2), :] = far1[Y1 * 32 : Y1 * 32 + 32, part] * 0.5
    high, low = split(h_ref[0, 0, 0:32, :])
    made = dot3(high, low, twice_high[:, :128], twice_low[:, :128])
    local2 = jnp.where(parity == 1, made[:, 256:512], made[:, 0:256])
    half = lanes((32, 128)) // 64
    for Y1 in range(2):
        for tz in range(2):
            part = jnp.where(half == tz, local2[:, Y1 * 128 : Y1 * 128 + 128], 0.0)
            h_ref[1, 1, pl.ds(Y1 * 64 + tz, 32, stride=2), :] = part
    high, low = split(jnp.concatenate([h_ref[1, 0], h_ref[1, 1]], axis=1))
    l1_ref[...] = dot3(high, low, twice_high, twice_low)

    for dx in SIDES:
        arrive(leaf_x[dx, 2])
        for dy in SIDES:
            arrive(leaf_xy[dx, dy])
    sums = []
    for mz in range(3):
        lower = upper = None
        for my in range(3):
            made = dot_nt(src0[0, my : my + 4].reshape(256, 256), weight(0, my, mz))
            lower = made if lower is None else lower + made
            made = dot_nt(src0[3, my : my + 4].reshape(256, 256), weight(2, my, mz))
            upper = made if upper is None else upper + made
        sums.append(acc_ref[mz] + jnp.concatenate([lower, upper], axis=0))
    far_ref[...] = shifted(sums, 64)

    half = lanes((64, 128)) // 64
    woven = lanes((64, 128))
    woven = (woven & 1) * 64 + (woven >> 1)
    for X in range(2):
        for Y1 in range(2):
            far, local = [], []
            for ty in range(2):
                parent = X * 4 + 2 * Y1 + ty
                above = l1_ref[Y1 * 64 : Y1 * 64 + 64, (X * 2 + ty) * 128 : (X * 2 + ty) * 128 + 128]
                for tz in range(2):
                    part = slice(128, 256) if tz == 0 else slice(0, 128)
                    far.append(far_ref[parent * 64 : parent * 64 + 64, part])
                    local.append(jnp.where(half == tz, above, 0.0))
            high, low = split(jnp.concatenate([jnp.concatenate(far, axis=0), jnp.concatenate(local, axis=0)], axis=1))
            made = dot3(wd_high, wd_low, high, low)
            for Y in range(2):
                for tx in range(2):
                    for ty in range(2):
                        piece = made[(2 * tx + ty) * 64 : (2 * tx + ty) * 64 + 64, Y * 128 : Y * 128 + 128]
                        piece = jnp.take_along_axis(piece, woven, axis=1)
                        out_ref[pl.ds((2 * X + tx) * 8 + 4 * Y1 + 2 * Y + ty, 64, stride=32), :] = piece
    for going, copy in waits:
        pl.when(going)(copy.wait_send)


def per_device(leaf_multipoles, m2l_ops, proj_in, proj_out, m2m, n_gx, n_gy):
    vmem = pl.BlockSpec(memory_space=pltpu.VMEM)
    hbm = pl.BlockSpec(memory_space=pltpu.HBM)
    made = pl.pallas_call(
        functools.partial(kernel, n_gx, n_gy),
        out_shape=jax.ShapeDtypeStruct((2048, 128), F32),
        in_specs=[hbm] * 5,
        out_specs=vmem,
        scratch_shapes=[
            pltpu.VMEM((32, 64), F32),
            pltpu.VMEM((32, 64), F32),
            pltpu.VMEM((8, 64, 64), F32),
            pltpu.VMEM((2, 64, 16, 128), F32),
            pltpu.VMEM((32, 32, 316), BF16),
            pltpu.VMEM((344 * 8, 128), F32),
            pltpu.VMEM((8, 2, 128, 128), F32),
            pltpu.VMEM((2, 512, 256), BF16),
            pltpu.VMEM((2, 512, 256), BF16),
            pltpu.VMEM((512, 128), F32),
            pltpu.VMEM((64, 128), F32),
            pltpu.VMEM((4, 6, 64, 256), BF16),
            pltpu.VMEM((3, 4, 32, 256), BF16),
            pltpu.VMEM((3, 6, 16, 128), BF16),
            pltpu.VMEM((3, 3, 7, 128, 128), BF16),
            pltpu.VMEM((2, 2, 192, 256), BF16),
            pltpu.VMEM((2, 256, 256), BF16),
            pltpu.VMEM((3, 512, 256), F32),
            pltpu.VMEM((512, 256), F32),
            pltpu.VMEM((2, 2, 128, 128), F32),
            pltpu.VMEM((128, 512), F32),
            pltpu.SemaphoreType.DMA((2,)),
            pltpu.SemaphoreType.DMA,
            pltpu.SemaphoreType.DMA((3,)),
            pltpu.SemaphoreType.DMA((MESSAGES,)),
            pltpu.SemaphoreType.DMA((MESSAGES,)),
            pltpu.SemaphoreType.DMA((6,)),
        ],
        compiler_params=pltpu.CompilerParams(
            collective_id=0, has_side_effects=True, vmem_limit_bytes=48 * 1024 * 1024
        ),
        name="far_field",
    )
    operands = (leaf_multipoles.reshape(64, 32, 128), m2l_ops.transpose(1, 2, 0), proj_in, proj_out.T, m2m)
    made = made(*(pltpu.with_memory_space_constraint(operand, pltpu.HBM) for operand in operands))
    return made.reshape(leaf_multipoles.shape)


def solution(mesh):
    placed = (P(None, "gx", "gy", None), P(), P(), P(), P())
    return jax.shard_map(
        functools.partial(per_device, n_gx=mesh.shape["gx"], n_gy=mesh.shape["gy"]),
        mesh=mesh,
        in_specs=placed,
        out_specs=P(None, "gx", "gy", None),
        check_vma=False,
    )
```

time: 28.2 us -> 20.9 us (0.74)
  the two profiles are of different devices: /device:TPU:109 before, /device:TPU:129 now
where the time goes in v2:
time: 20.9 us; the launch traced here: 20.7 us
  Pallas kernels  19.8 us (95%)
  local copies, waits for them, and re-layouts  0.97 us (5%)
    pallas_call x1, Pallas kernels, per_device(): made(*(pltpu.with_memory_space_constraint(operand, pltpu.HBM) for operand...  19.8 us
    unnamed x1, local copies, waits for them, and re-layouts  0.97 us

profile of v2, /device:TPU:129, one launch (start us, length us, event | category | flops | bytes accessed | tf_op | source)
XLA Modules:
  0.0 20.7 jit_solution(2455245955401667288)
XLA Ops:
  0.0 19.8 %far_field.1 = f32[2048,128]{1,0:T(8,128)S(1)} custom-call(f32[64,32,128]{2,1,0:T(8,128)} %bitcast.5, bf16[32,32,316]{2,1,0:T(8,128)(2,1)} %bitcast.6, f32[32,64]{1,0:T(8,128)} %pin_hbm.1, f32[32,64]{1,0:T(8,128)} %bitcast.7, f32[8,64,64]{2,1,0:T(8,128)} %m2m_hbm.1), custom_call_target="tpu_custom_call" | custom-call | tf_op jit(solution)/shard_map/far_field/pallas_call | solution.py:474
  19.8 1.0 %copy.7 = f32[64,4,8,128]{3,2,1,0:T(8,128)} copy(f32[64,4,8,128]{3,2,1,0:T(8,128)S(1)} %bitcast.4) | data formatting | bytes 2097152

commit v3 on v2

--- a/solution.py
+++ b/solution.py
@@ -37,12 +37,39 @@
 MESSAGES = 27
 
 
+def moved(value, step):
+    at_end = 15 if step == 1 else 0
+    turned = pltpu.roll(value, value.shape[0] - 1 if step == 1 else 1, 0)
+    return jnp.where(rows(value.shape) & 15 == at_end, 0.0, turned)
+
+
+def seen_from(value, step, blocks):
+    count, width = value.shape
+    parts = value.reshape(count // (16 * blocks), blocks, 16, width)
+    parts = [parts[:, k] for k in range(blocks)]
+
+    def edge(part):
+        return moved(part.reshape(-1, width), step).reshape(part.shape)
+
+    if step == 1:
+        parts = {1: lambda: [edge(parts[0])], 2: lambda: [parts[1], edge(parts[0])],
+                 4: lambda: [parts[2], parts[3], parts[1], edge(parts[0])]}[blocks]()
+    else:
+        parts = {1: lambda: [edge(parts[0])], 2: lambda: [edge(parts[1]), parts[0]],
+                 4: lambda: [edge(parts[3]), parts[2], parts[0], parts[1]]}[blocks]()
+    return jnp.stack(parts, axis=1).reshape(count, width)
+
+
+def shifted(sums, blocks):
+    return sums[1] + seen_from(sums[0], -1, blocks) + seen_from(sums[2], 1, blocks)
+
+
 def kernel(
     n_gx, n_gy,
     x_hbm, ops_hbm, pin_hbm, pout_hbm, m2m_hbm,
     out_ref,
-    pin_ref, pout_ref, m2m_ref, x_ref, ops_ref, wide_ref, turn_ref, dh_ref, dl_ref, m1_ref, m2_ref, src0, src1, cin, q_ref,
-    wup_ref, wd_ref, acc_ref, far_ref, h_ref, l1_ref,
+    pin_ref, pout_ref, m2m_ref, x_ref, ops_ref, wide_ref, turn_ref, dh_ref, dl_ref, src0, src1, cin, q_ref,
+    wup_ref, wd_ref, acc_ref, stage_ref,
     in_sem, ops_sem, weight_sem, sent, came, coarse_came,
 ):
     px, py = lax.axis_index("gx"), lax.axis_index("gy")
@@ -50,11 +77,16 @@
     far_dx = 3 - 6 * parity
 
     def device(dx, dy):
-        return (lax.rem(px + (dx + n_gx), n_gx), lax.rem(py + (dy + n_gy), n_gy))
+        return (px + dx, py + dy)
+
+    inside = {
+        (1, 0): px < n_gx - 1, (-1, 0): px > 0, (2, 0): px < n_gx - 2, (-2, 0): px > 1,
+        (0, 1): py < n_gy - 1, (0, -1): py > 0,
+    }
+    far_inside = (parity == 0) & (px < n_gx - 3) | (parity == 1) & (px > 2)
 
     def exists(dx, dy):
-        x, y = px + dx, py + dy
-        return (x >= 0) & (x < n_gx) & (y >= 0) & (y < n_gy)
+        return inside[dx, dy] if isinstance(dx, int) else far_inside
 
     weight_copies = [
         pltpu.make_async_copy(source, target, weight_sem.at[k])
@@ -63,7 +95,7 @@
     for copy in weight_copies:
         copy.start()
     x_copies = [
-        pltpu.make_async_copy(x_hbm.at[:, pl.ds(16 * X, 16)], x_ref.at[X], in_sem.at[X]) for X in range(2)
+        pltpu.make_async_copy(x_hbm.at[:, pl.ds(16 * X, 16)], x_ref.at[X, :, pl.ds(0, 16)], in_sem.at[X]) for X in range(2)
     ]
     for copy in x_copies:
         copy.start()
@@ -96,7 +128,8 @@
 
     barrier = pltpu.get_barrier_semaphore()
     greeted = 0
-    for dx, dy in ((1, 0), (-1, 0), (0, 1), (0, -1), (2, 0), (-2, 0), (far_dx, 0)):
+    coarse_moves = [(far_dx, 0), (2, 0), (-2, 0), (1, 0), (-1, 0)]
+    for dx, dy in coarse_moves + [(0, 1), (0, -1)]:
         greeted = greeted + exists(dx, dy).astype(jnp.int32)
 
         @pl.when(exists(dx, dy))
@@ -150,21 +183,22 @@
             mid_xy[dx, dy] = message(src1.at[1 - dx, row1], src1.at[1 - dx, halo1], 0, dy, -dx)
     coarse_x = []
     own = cin.at[1, 2 + parity]
-    for dx in (far_dx, 2, -2, 1, -1):
+    for dx, dy in coarse_moves:
         slot = (2 - dx) + lax.rem(px + (dx + n_gx), 2)
-        coarse_x.append(message(own, cin.at[1, slot], dx, 0, came_sem=coarse_came.at[slot]))
+        target = cin.at[1 - dy, slot]
+        coarse_x.append(message(own, target, dx, dy, came_sem=coarse_came.at[1 - dy, slot]))
     coarse_arrivals = []
-    for k, dx in enumerate((far_dx, 2, -2, 1, -1)):
+    for dx, dy in coarse_moves:
         slot = dx + 2 + parity
         copy = pltpu.make_async_remote_copy(
             src_ref=own,
-            dst_ref=cin.at[1, slot],
+            dst_ref=cin.at[1 + dy, slot],
             send_sem=sent.at[0],
-            recv_sem=coarse_came.at[slot],
-            device_id=device(dx, 0),
+            recv_sem=coarse_came.at[1 + dy, slot],
+            device_id=device(dx, dy),
             device_id_type=MESH,
         )
-        coarse_arrivals.append((copy, None, exists(dx, 0)))
+        coarse_arrivals.append((copy, None, exists(dx, dy)))
 
     for copy in weight_copies:
         copy.wait()
@@ -179,14 +213,14 @@
         wup_ref[sz, 0] = high
         wup_ref[sz, 1] = low
 
-    flat_ref = x_ref.reshape(2048, 128)
+    flat_ref = x_ref.reshape(3072, 128)
     for X in range(2):
         x_copies[X].wait()
         for Y in range(4):
             parent = X * 4 + Y
             block = jnp.concatenate(
                 [
-                    flat_ref[pl.ds(X * 1024 + sx * 8 + 2 * Y + sy, 64, stride=16), :]
+                    flat_ref[pl.ds(X * 1536 + sx * 8 + 2 * Y + sy, 64, stride=24), :]
                     for sx in range(2)
                     for sy in range(2)
                 ],
@@ -198,36 +232,30 @@
             for sz in range(2):
                 high, low = split(
                     jnp.concatenate(
-                        [turn_ref[parent, sx, pl.ds(sz, 64, stride=2), :] for sx in range(2)], axis=1
+                        [
+                            jnp.concatenate(
+                                [turn_ref[parent, sx, pl.ds(sz + bits, 16, stride=8), :] for bits in (0, 4, 2, 6)],
+                                axis=0,
+                            )
+                            for sx in range(2)
+                        ],
+                        axis=1,
                     )
                 )
                 dh_ref[sz, pl.ds(parent * 64, 64)] = high
                 dl_ref[sz, pl.ds(parent * 64, 64)] = low
+
     total = None
     for sz in range(2):
         made = dot3(dh_ref[sz], dl_ref[sz], wup_ref[sz, 0], wup_ref[sz, 1])
         src0[1:3, 1:5, :, sz * 128 : (sz + 1) * 128] = made[:, :128].astype(BF16).reshape(2, 4, 64, 128)
         total = made[:, 128:] if sz == 0 else total + made[:, 128:]
-    m1_ref[:, 0:64] = total
-    pl.semaphore_wait(barrier, greeted)
-    for first in (4, 1, 2):
-        for dx in SIDES:
-            start(leaf_x[dx, first])
-    for dy in SIDES:
-        start(leaf_y[dy])
-
+    level1 = total.reshape(2, 4, 2, 32, 64)
     total = None
     for sz in range(2):
         block = jnp.concatenate(
             [
-                jnp.concatenate(
-                    [
-                        m1_ref[pl.ds((sx * 4 + 2 * Y1 + sy) * 64 + sz, 32, stride=2), :][:, 0:64]
-                        for sx in range(2)
-                        for sy in range(2)
-                    ],
-                    axis=1,
-                )
+                jnp.concatenate([level1[sx, 2 * Y1 + sy, sz] for sx in range(2) for sy in range(2)], axis=1)
                 for Y1 in range(2)
             ],
             axis=0,
@@ -236,22 +264,24 @@
         made = dot3(high, low, wup_ref[sz, 0], wup_ref[sz, 1])
         src1[1, 1:3, :, sz * 128 : (sz + 1) * 128] = made[:, :128].astype(BF16).reshape(2, 32, 128)
         total = made[:, 128:] if sz == 0 else total + made[:, 128:]
-    m2_ref[:, 0:64] = total
+    level2 = total.reshape(2, 2, 16, 64)
+    pieces = []
+    for sz in range(2):
+        high, low = split(jnp.concatenate([level2[0, sz], level2[1, sz]], axis=1))
+        pieces.append(dot3(high, low, wup_ref[0, 0, 0:64, 0:128], wup_ref[0, 1, 0:64, 0:128]))
+    cin[1, 2 + parity] = jnp.concatenate(pieces, axis=1).astype(BF16)
+    pl.semaphore_wait(barrier, greeted)
+    for item in coarse_x:
+        start(item)
     for dx in SIDES:
         start(mid_x[dx])
     for dy in SIDES:
         start(mid_y[dy])
-
-    pieces = []
-    for sz in range(2):
-        pair = jnp.concatenate(
-            [m2_ref[pl.ds(sy * 32 + sz, 16, stride=2), :][:, 0:64] for sy in range(2)], axis=1
-        )
-        high, low = split(pair)
-        pieces.append(dot3(high, low, wup_ref[0, 0, 0:64, 0:128], wup_ref[0, 1, 0:64, 0:128]))
-    cin[1, 2 + parity] = jnp.concatenate(pieces, axis=1).astype(BF16)
-    for item in coarse_x:
-        start(item)
+    for first in (4, 1, 2):
+        for dx in SIDES:
+            start(leaf_x[dx, first])
+    for dy in SIDES:
+        start(leaf_y[dy])
 
     position, number = rows((344, 316)), lanes((344, 316))
     ox, oy, oz = position // 49, position // 7 % 7, position % 7
@@ -267,19 +297,6 @@
         made = dot_nt(pick, slab)
         wide_ref[pair * 688 : pair * 688 + 344, :] = made[:, :128]
         wide_ref[pair * 688 + 344 : pair * 688 + 688, :] = made[:, 128:]
-
-    for first in (4, 1):
-        for dx in SIDES:
-            arrive(leaf_x[dx, first])
-            start(leaf_xy[dx, 1 if first == 4 else -1])
-    for dx in SIDES:
-        arrive(mid_x[dx])
-        for dy in SIDES:
-            start(mid_xy[dx, dy])
-    for item in coarse_arrivals:
-        arrive(item)
-    for dy in SIDES:
-        start(coarse_y[dy])
 
     place = lanes((8, 128)) // 32
 
@@ -321,13 +338,14 @@
             axis=1,
         )
 
-    def shifted(sums, size):
-        inner = rows(sums[0].shape) & (size - 1)
-        count = sums[0].shape[0]
-        below = jnp.where(inner == 0, 0.0, pltpu.roll(sums[0], 1, 0))
-        above = jnp.where(inner == size - 1, 0.0, pltpu.roll(sums[2], count - 1, 0))
-        return sums[1] + below + above
-
+    for item in coarse_arrivals:
+        arrive(item)
+    for dy in SIDES:
+        start(coarse_y[dy])
+    for dx in SIDES:
+        arrive(mid_x[dx])
+        for dy in SIDES:
+            start(mid_xy[dx, dy])
     for dy in SIDES:
         arrive(leaf_y[dy])
     for mz in range(3):
@@ -340,9 +358,28 @@
             acc = made if acc is None else acc + made
         acc_ref[mz] = acc
 
+    for first in (4, 1):
+        for dx in SIDES:
+            arrive(leaf_x[dx, first])
+            start(leaf_xy[dx, 1 if first == 4 else -1])
+
+    for dx in SIDES:
+        arrive(leaf_x[dx, 2])
+    empty = jnp.zeros((64, 256), F32)
+    for mz in range(3):
+        sides = []
+        for mx, column in ((0, 0), (2, 3)):
+            middle = dot_nt(src0[column, 1:5].reshape(256, 256), weight(mx, 1, mz))
+            before = dot_nt(src0[column, 1:4].reshape(192, 256), weight(mx, 0, mz))
+            after = dot_nt(src0[column, 2:5].reshape(192, 256), weight(mx, 2, mz))
+            made = middle + jnp.concatenate([empty, before], axis=0) + jnp.concatenate([after, empty], axis=0)
+            sides.append(made)
+        acc_ref[mz] += jnp.concatenate(sides, axis=0)
+
+    for dy in SIDES:
+        arrive(coarse_y[dy])
     for dy in SIDES:
         arrive(mid_y[dy])
-        arrive(coarse_y[dy])
         for dx in SIDES:
             arrive(mid_xy[dx, dy])
     sums = []
@@ -356,8 +393,8 @@
                 made = dot_nt(source, weight(mx, my, mz))
                 acc = made if acc is None else acc + made
         sums.append(acc)
-    far1 = shifted([acc[0:64] for acc in sums], 32)
-    far2 = shifted([acc[64:80] for acc in sums], 16)
+    far1 = shifted([acc[0:64] for acc in sums], 2)
+    far2 = shifted([acc[64:80] for acc in sums], 1)
 
     pout = pout_ref[...].T
     pout2 = jnp.concatenate([pout, pout], axis=1)
@@ -372,58 +409,53 @@
     twice_high = jnp.concatenate([wd_high[k * 64 : k * 64 + 64] for k in (0, 0, 1, 1, 2, 2, 3, 3)], axis=0)
     twice_low = jnp.concatenate([wd_low[k * 64 : k * 64 + 64] for k in (0, 0, 1, 1, 2, 2, 3, 3)], axis=0)
 
-    for tz in range(2):
-        part = slice(128, 256) if tz == 0 else slice(0, 128)
-        h_ref[0, 0, pl.ds(tz, 16, stride=2), :] = far2[:, part] * 0.25
-        for Y1 in range(2):
-            h_ref[1, 0, pl.ds(Y1 * 64 + tz, 32, stride=2), :] = far1[Y1 * 32 : Y1 * 32 + 32, part] * 0.5
-    high, low = split(h_ref[0, 0, 0:32, :])
+    high, low = split(jnp.concatenate([far2[:, 128:256], far2[:, 0:128]], axis=0) * 0.25)
     made = dot3(high, low, twice_high[:, :128], twice_low[:, :128])
     local2 = jnp.where(parity == 1, made[:, 256:512], made[:, 0:256])
-    half = lanes((32, 128)) // 64
-    for Y1 in range(2):
-        for tz in range(2):
-            part = jnp.where(half == tz, local2[:, Y1 * 128 : Y1 * 128 + 128], 0.0)
-            h_ref[1, 1, pl.ds(Y1 * 64 + tz, 32, stride=2), :] = part
-    high, low = split(jnp.concatenate([h_ref[1, 0], h_ref[1, 1]], axis=1))
-    l1_ref[...] = dot3(high, low, twice_high, twice_low)
+    def beside(local):
+        first = lanes(local.shape) < 64
+        return jnp.concatenate([jnp.where(first, local, 0.0), jnp.where(first, 0.0, local)], axis=0)
+
+    far1 = far1.reshape(2, 32, 256) * 0.5
+    far1 = jnp.concatenate([far1[Y1, :, part] for Y1 in range(2) for part in (slice(128, 256), slice(0, 128))], axis=0)
+    local = jnp.concatenate([beside(local2[:, Y1 * 128 : Y1 * 128 + 128]) for Y1 in range(2)], axis=0)
+    high, low = split(jnp.concatenate([far1, local], axis=1))
+    local1 = dot3(high, low, twice_high, twice_low)
 
     for dx in SIDES:
-        arrive(leaf_x[dx, 2])
         for dy in SIDES:
             arrive(leaf_xy[dx, dy])
     sums = []
     for mz in range(3):
-        lower = upper = None
-        for my in range(3):
-            made = dot_nt(src0[0, my : my + 4].reshape(256, 256), weight(0, my, mz))
-            lower = made if lower is None else lower + made
-            made = dot_nt(src0[3, my : my + 4].reshape(256, 256), weight(2, my, mz))
-            upper = made if upper is None else upper + made
-        sums.append(acc_ref[mz] + jnp.concatenate([lower, upper], axis=0))
-    far_ref[...] = shifted(sums, 64)
-
-    half = lanes((64, 128)) // 64
-    woven = lanes((64, 128))
-    woven = (woven & 1) * 64 + (woven >> 1)
+        parts = []
+        for mx, column in ((0, 0), (2, 3)):
+            before = dot_nt(src0[column, 0], weight(mx, 0, mz))
+            after = dot_nt(src0[column, 5], weight(mx, 2, mz))
+            parts += [before, jnp.zeros((128, 256), F32), after]
+        sums.append(acc_ref[mz] + jnp.concatenate(parts, axis=0))
+    far0 = shifted(sums, 4)
+
+    place = lanes((64, 128))
+    woven = (place & 1) * 64 + (place >> 1 & 1) * 32 + (place >> 2 & 1) * 16 + (place >> 3)
     for X in range(2):
         for Y1 in range(2):
             far, local = [], []
             for ty in range(2):
                 parent = X * 4 + 2 * Y1 + ty
-                above = l1_ref[Y1 * 64 : Y1 * 64 + 64, (X * 2 + ty) * 128 : (X * 2 + ty) * 128 + 128]
-                for tz in range(2):
-                    part = slice(128, 256) if tz == 0 else slice(0, 128)
-                    far.append(far_ref[parent * 64 : parent * 64 + 64, part])
-                    local.append(jnp.where(half == tz, above, 0.0))
+                for part in (slice(128, 256), slice(0, 128)):
+                    far.append(far0[parent * 64 : parent * 64 + 64, part])
+                local.append(beside(local1[Y1 * 64 : Y1 * 64 + 64, (X * 2 + ty) * 128 : (X * 2 + ty) * 128 + 128]))
             high, low = split(jnp.concatenate([jnp.concatenate(far, axis=0), jnp.concatenate(local, axis=0)], axis=1))
             made = dot3(wd_high, wd_low, high, low)
             for Y in range(2):
                 for tx in range(2):
                     for ty in range(2):
                         piece = made[(2 * tx + ty) * 64 : (2 * tx + ty) * 64 + 64, Y * 128 : Y * 128 + 128]
-                        piece = jnp.take_along_axis(piece, woven, axis=1)
-                        out_ref[pl.ds((2 * X + tx) * 8 + 4 * Y1 + 2 * Y + ty, 64, stride=32), :] = piece
+                        first = ((2 * X + tx) * 8 + 4 * Y1 + 2 * Y + ty) * 72
+                        stage_ref[first : first + 64, :] = jnp.take_along_axis(piece, woven, axis=1)
+        for x in (2 * X, 2 * X + 1):
+            for c in range(64):
+                out_ref[c * 32 + x * 8 : c * 32 + x * 8 + 8, :] = stage_ref[pl.ds(x * 576 + c, 8, stride=72), :]
     for going, copy in waits:
         pl.when(going)(copy.wait_send)
 
@@ -440,14 +472,12 @@
             pltpu.VMEM((32, 64), F32),
             pltpu.VMEM((32, 64), F32),
             pltpu.VMEM((8, 64, 64), F32),
-            pltpu.VMEM((2, 64, 16, 128), F32),
+            pltpu.VMEM((2, 64, 24, 128), F32),
             pltpu.VMEM((32, 32, 316), BF16),
             pltpu.VMEM((344 * 8, 128), F32),
             pltpu.VMEM((8, 2, 128, 128), F32),
             pltpu.VMEM((2, 512, 256), BF16),
             pltpu.VMEM((2, 512, 256), BF16),
-            pltpu.VMEM((512, 128), F32),
-            pltpu.VMEM((64, 128), F32),
             pltpu.VMEM((4, 6, 64, 256), BF16),
             pltpu.VMEM((3, 4, 32, 256), BF16),
             pltpu.VMEM((3, 6, 16, 128), BF16),
@@ -455,15 +485,13 @@
             pltpu.VMEM((2, 2, 192, 256), BF16),
             pltpu.VMEM((2, 256, 256), BF16),
             pltpu.VMEM((3, 512, 256), F32),
-            pltpu.VMEM((512, 256), F32),
-            pltpu.VMEM((2, 2, 128, 128), F32),
-            pltpu.VMEM((128, 512), F32),
+            pltpu.VMEM((32 * 72, 128), F32),
             pltpu.SemaphoreType.DMA((2,)),
             pltpu.SemaphoreType.DMA,
             pltpu.SemaphoreType.DMA((3,)),
             pltpu.SemaphoreType.DMA((MESSAGES,)),
             pltpu.SemaphoreType.DMA((MESSAGES,)),
-            pltpu.SemaphoreType.DMA((6,)),
+            pltpu.SemaphoreType.DMA((3, 6)),
         ],
         compiler_params=pltpu.CompilerParams(
             collective_id=0, has_side_effects=True, vmem_limit_bytes=48 * 1024 * 1024

time: 20.9 us -> 19.5 us (0.933)
  the two profiles are of different devices: /device:TPU:129 before, /device:TPU:152 now
where the time goes in v3:
time: 19.5 us; the launch traced here: 19.3 us
  Pallas kernels  18.3 us (94%)
  local copies, waits for them, and re-layouts  0.97 us (5%)
    pallas_call x1, Pallas kernels, per_device(): made(*(pltpu.with_memory_space_constraint(operand, pltpu.HBM) for operand...  18.3 us
    unnamed x1, local copies, waits for them, and re-layouts  0.97 us

profile of v3, /device:TPU:152, one launch (start us, length us, event | category | flops | bytes accessed | tf_op | source)
XLA Modules:
  0.0 19.3 jit_solution(3774468161152506913)
XLA Ops:
  0.0 18.3 %far_field.1 = f32[2048,128]{1,0:T(8,128)S(1)} custom-call(f32[64,32,128]{2,1,0:T(8,128)} %bitcast.5, bf16[32,32,316]{2,1,0:T(8,128)(2,1)} %bitcast.6, f32[32,64]{1,0:T(8,128)} %pin_hbm.1, f32[32,64]{1,0:T(8,128)} %bitcast.7, f32[8,64,64]{2,1,0:T(8,128)} %m2m_hbm.1), custom_call_target="tpu_custom_call" | custom-call | tf_op jit(solution)/shard_map/far_field/pallas_call | solution.py:502
  18.3 1.0 %copy.7 = f32[64,4,8,128]{3,2,1,0:T(8,128)} copy(f32[64,4,8,128]{3,2,1,0:T(8,128)S(1)} %bitcast.4) | data formatting | bytes 2097152

commit v4 on v3

--- a/solution.py
+++ b/solution.py
@@ -69,7 +69,7 @@
     x_hbm, ops_hbm, pin_hbm, pout_hbm, m2m_hbm,
     out_ref,
     pin_ref, pout_ref, m2m_ref, x_ref, ops_ref, wide_ref, turn_ref, dh_ref, dl_ref, src0, src1, cin, q_ref,
-    wup_ref, wd_ref, acc_ref, stage_ref,
+    wup_ref, wd_ref, acc_ref, acc1_ref, stage_ref,
     in_sem, ops_sem, weight_sem, sent, came, coarse_came,
 ):
     px, py = lax.axis_index("gx"), lax.axis_index("gy")
@@ -338,6 +338,24 @@
             axis=1,
         )
 
+    for dy in SIDES:
+        arrive(leaf_y[dy])
+        arrive(mid_y[dy])
+    for mz in range(3):
+        acc = acc1 = None
+        for my in range(3):
+            source = jnp.concatenate(
+                [src0[1:3, my : my + 4].reshape(512, 256), src1[1, my : my + 2].reshape(64, 256)], axis=0
+            )
+            both = dot_nt(source, weight(1, my, mz))
+            lower = dot_nt(src0[2, my : my + 4].reshape(256, 256), weight(2, my, mz))
+            upper = dot_nt(src0[1, my : my + 4].reshape(256, 256), weight(0, my, mz))
+            made = both[0:512] + jnp.concatenate([lower, upper], axis=0)
+            acc = made if acc is None else acc + made
+            acc1 = both[512:] if acc1 is None else acc1 + both[512:]
+        acc_ref[mz] = acc
+        acc1_ref[mz] = acc1
+
     for item in coarse_arrivals:
         arrive(item)
     for dy in SIDES:
@@ -346,18 +364,6 @@
         arrive(mid_x[dx])
         for dy in SIDES:
             start(mid_xy[dx, dy])
-    for dy in SIDES:
-        arrive(leaf_y[dy])
-    for mz in range(3):
-        acc = None
-        for my in range(3):
-            both = dot_nt(src0[1:3, my : my + 4].reshape(512, 256), weight(1, my, mz))
-            lower = dot_nt(src0[2, my : my + 4].reshape(256, 256), weight(2, my, mz))
-            upper = dot_nt(src0[1, my : my + 4].reshape(256, 256), weight(0, my, mz))
-            made = both + jnp.concatenate([lower, upper], axis=0)
-            acc = made if acc is None else acc + made
-        acc_ref[mz] = acc
-
     for first in (4, 1):
         for dx in SIDES:
             arrive(leaf_x[dx, first])
@@ -368,33 +374,21 @@
     empty = jnp.zeros((64, 256), F32)
     for mz in range(3):
         sides = []
+        mids = acc1_ref[mz]
         for mx, column in ((0, 0), (2, 3)):
-            middle = dot_nt(src0[column, 1:5].reshape(256, 256), weight(mx, 1, mz))
-            before = dot_nt(src0[column, 1:4].reshape(192, 256), weight(mx, 0, mz))
-            after = dot_nt(src0[column, 2:5].reshape(192, 256), weight(mx, 2, mz))
-            made = middle + jnp.concatenate([empty, before], axis=0) + jnp.concatenate([after, empty], axis=0)
-            sides.append(made)
+            source = jnp.concatenate(
+                [src0[column, 1:5].reshape(256, 256), src1[mx, 1:3].reshape(64, 256)], axis=0
+            )
+            middle = dot_nt(source, weight(mx, 1, mz))
+            source = jnp.concatenate([src0[column, 1:4].reshape(192, 256), src1[mx, 1]], axis=0)
+            before = dot_nt(source, weight(mx, 0, mz))
+            source = jnp.concatenate([src0[column, 2:5].reshape(192, 256), src1[mx, 2]], axis=0)
+            after = dot_nt(source, weight(mx, 2, mz))
+            made = middle[0:256] + jnp.concatenate([empty, before[0:192]], axis=0)
+            sides.append(made + jnp.concatenate([after[0:192], empty], axis=0))
+            mids = mids + (middle[256:320] + jnp.concatenate([after[192:224], before[192:224]], axis=0))
         acc_ref[mz] += jnp.concatenate(sides, axis=0)
-
-    for dy in SIDES:
-        arrive(coarse_y[dy])
-    for dy in SIDES:
-        arrive(mid_y[dy])
-        for dx in SIDES:
-            arrive(mid_xy[dx, dy])
-    sums = []
-    for mz in range(3):
-        acc = None
-        for mx in range(3):
-            for my in range(3):
-                one, two = cin[my, 2 * mx], cin[my, 2 * mx + 1]
-                coarse = jnp.concatenate([one[:, :64], two[:, :64], one[:, 64:], two[:, 64:]], axis=1)
-                source = jnp.concatenate([src1[mx, my : my + 2].reshape(64, 256), coarse], axis=0)
-                made = dot_nt(source, weight(mx, my, mz))
-                acc = made if acc is None else acc + made
-        sums.append(acc)
-    far1 = shifted([acc[0:64] for acc in sums], 2)
-    far2 = shifted([acc[64:80] for acc in sums], 1)
+        acc1_ref[mz] = mids
 
     pout = pout_ref[...].T
     pout2 = jnp.concatenate([pout, pout], axis=1)
@@ -409,9 +403,36 @@
     twice_high = jnp.concatenate([wd_high[k * 64 : k * 64 + 64] for k in (0, 0, 1, 1, 2, 2, 3, 3)], axis=0)
     twice_low = jnp.concatenate([wd_low[k * 64 : k * 64 + 64] for k in (0, 0, 1, 1, 2, 2, 3, 3)], axis=0)
 
-    high, low = split(jnp.concatenate([far2[:, 128:256], far2[:, 0:128]], axis=0) * 0.25)
-    made = dot3(high, low, twice_high[:, :128], twice_low[:, :128])
-    local2 = jnp.where(parity == 1, made[:, 256:512], made[:, 0:256])
+    for dy in SIDES:
+        arrive(coarse_y[dy])
+        for dx in SIDES:
+            arrive(mid_xy[dx, dy])
+    own_side = pl.ds(pl.multiple_of(parity * 64, 64), 64)
+    acc = None
+    for mx in range(3):
+        for my in range(3):
+            one, two = cin[my, 2 * mx], cin[my, 2 * mx + 1]
+            coarse = jnp.concatenate([one[:, :64], two[:, :64], one[:, 64:], two[:, 64:]], axis=1)
+            wanted = jnp.concatenate(
+                [
+                    q_ref[mx, my, 0:6, own_side].reshape(384, 128),
+                    q_ref[mx, my, 1:7, own_side].reshape(384, 128),
+                ],
+                axis=1,
+            )
+            made = dot_nt(coarse, wanted)
+            acc = made if acc is None else acc + made
+    far2 = shifted([acc[:, mz * 128 : mz * 128 + 128] for mz in range(3)], 1)
+    sums = []
+    for mz in range(3):
+        parts = []
+        for my, row in ((0, 0), (2, 3)):
+            parts.append(dot_nt(src1[0, row], weight(0, my, mz)) + dot_nt(src1[2, row], weight(2, my, mz)))
+        sums.append(acc1_ref[mz] + jnp.concatenate(parts, axis=0))
+    far1 = shifted(sums, 2)
+
+    high, low = split(jnp.concatenate([far2[:, 64:128], far2[:, 0:64]], axis=0) * 0.25)
+    local2 = dot3(high, low, twice_high[0:256, 0:64], twice_low[0:256, 0:64])
     def beside(local):
         first = lanes(local.shape) < 64
         return jnp.concatenate([jnp.where(first, local, 0.0), jnp.where(first, 0.0, local)], axis=0)
@@ -422,37 +443,39 @@
     high, low = split(jnp.concatenate([far1, local], axis=1))
     local1 = dot3(high, low, twice_high, twice_low)
 
+    place = lanes((64, 128))
+    woven = (place & 1) * 64 + (place >> 1 & 1) * 32 + (place >> 2 & 1) * 16 + (place >> 3)
+
+    def leaf_down(X, pair, far0):
+        far, local = [], []
+        for k, Y in enumerate(pair):
+            for part in (slice(128, 256), slice(0, 128)):
+                far.append(far0[k * 64 : k * 64 + 64, part])
+            Y1, ty = Y // 2, Y % 2
+            local.append(beside(local1[Y1 * 64 : Y1 * 64 + 64, (X * 2 + ty) * 128 : (X * 2 + ty) * 128 + 128]))
+        high, low = split(jnp.concatenate([jnp.concatenate(far, axis=0), jnp.concatenate(local, axis=0)], axis=1))
+        made = dot3(wd_high, wd_low, high, low)
+        for k, Y in enumerate(pair):
+            for tx in range(2):
+                for ty in range(2):
+                    piece = made[(2 * tx + ty) * 64 : (2 * tx + ty) * 64 + 64, k * 128 : k * 128 + 128]
+                    first = ((2 * X + tx) * 8 + 2 * Y + ty) * 72
+                    stage_ref[first : first + 64, :] = jnp.take_along_axis(piece, woven, axis=1)
+
+    for X in range(2):
+        first = X * 256 + 64
+        leaf_down(X, (1, 2), shifted([acc_ref[mz, first : first + 128] for mz in range(3)], 4))
+
     for dx in SIDES:
         for dy in SIDES:
             arrive(leaf_xy[dx, dy])
-    sums = []
-    for mz in range(3):
-        parts = []
-        for mx, column in ((0, 0), (2, 3)):
-            before = dot_nt(src0[column, 0], weight(mx, 0, mz))
-            after = dot_nt(src0[column, 5], weight(mx, 2, mz))
-            parts += [before, jnp.zeros((128, 256), F32), after]
-        sums.append(acc_ref[mz] + jnp.concatenate(parts, axis=0))
-    far0 = shifted(sums, 4)
-
-    place = lanes((64, 128))
-    woven = (place & 1) * 64 + (place >> 1 & 1) * 32 + (place >> 2 & 1) * 16 + (place >> 3)
-    for X in range(2):
-        for Y1 in range(2):
-            far, local = [], []
-            for ty in range(2):
-                parent = X * 4 + 2 * Y1 + ty
-                for part in (slice(128, 256), slice(0, 128)):
-                    far.append(far0[parent * 64 : parent * 64 + 64, part])
-                local.append(beside(local1[Y1 * 64 : Y1 * 64 + 64, (X * 2 + ty) * 128 : (X * 2 + ty) * 128 + 128]))
-            high, low = split(jnp.concatenate([jnp.concatenate(far, axis=0), jnp.concatenate(local, axis=0)], axis=1))
-            made = dot3(wd_high, wd_low, high, low)
-            for Y in range(2):
-                for tx in range(2):
-                    for ty in range(2):
-                        piece = made[(2 * tx + ty) * 64 : (2 * tx + ty) * 64 + 64, Y * 128 : Y * 128 + 128]
-                        first = ((2 * X + tx) * 8 + 4 * Y1 + 2 * Y + ty) * 72
-                        stage_ref[first : first + 64, :] = jnp.take_along_axis(piece, woven, axis=1)
+    for X, mx, column in ((0, 0, 0), (1, 2, 3)):
+        sums = []
+        for mz in range(3):
+            before = acc_ref[mz, X * 256 : X * 256 + 64] + dot_nt(src0[column, 0], weight(mx, 0, mz))
+            after = acc_ref[mz, X * 256 + 192 : X * 256 + 256] + dot_nt(src0[column, 5], weight(mx, 2, mz))
+            sums.append(jnp.concatenate([before, after], axis=0))
+        leaf_down(X, (0, 3), shifted(sums, 4))
         for x in (2 * X, 2 * X + 1):
             for c in range(64):
                 out_ref[c * 32 + x * 8 : c * 32 + x * 8 + 8, :] = stage_ref[pl.ds(x * 576 + c, 8, stride=72), :]
@@ -485,6 +508,7 @@
             pltpu.VMEM((2, 2, 192, 256), BF16),
             pltpu.VMEM((2, 256, 256), BF16),
             pltpu.VMEM((3, 512, 256), F32),
+            pltpu.VMEM((3, 64, 256), F32),
             pltpu.VMEM((32 * 72, 128), F32),
             pltpu.SemaphoreType.DMA((2,)),
             pltpu.SemaphoreType.DMA,

time: 19.5 us -> 18.4 us (0.944)
  the two profiles are of different devices: /device:TPU:152 before, /device:TPU:111 now
where the time goes in v4:
time: 18.4 us; the launch traced here: 18.3 us
  Pallas kernels  17.3 us (94%)
  local copies, waits for them, and re-layouts  0.97 us (5%)
    pallas_call x1, Pallas kernels, per_device(): made(*(pltpu.with_memory_space_constraint(operand, pltpu.HBM) for operand...  17.3 us
    unnamed x1, local copies, waits for them, and re-layouts  0.97 us

profile of v4, /device:TPU:111, one launch (start us, length us, event | category | flops | bytes accessed | tf_op | source)
XLA Modules:
  0.0 18.3 jit_solution(16837121726590483062)
XLA Ops:
  0.0 17.3 %far_field.1 = f32[2048,128]{1,0:T(8,128)S(1)} custom-call(f32[64,32,128]{2,1,0:T(8,128)} %bitcast.5, bf16[32,32,316]{2,1,0:T(8,128)(2,1)} %bitcast.6, f32[32,64]{1,0:T(8,128)} %pin_hbm.1, f32[32,64]{1,0:T(8,128)} %bitcast.7, f32[8,64,64]{2,1,0:T(8,128)} %m2m_hbm.1), custom_call_target="tpu_custom_call" | custom-call | tf_op jit(solution)/shard_map/far_field/pallas_call | solution.py:526
  17.3 1.0 %copy.7 = f32[64,4,8,128]{3,2,1,0:T(8,128)} copy(f32[64,4,8,128]{3,2,1,0:T(8,128)S(1)} %bitcast.4) | data formatting | bytes 2097152

commit v5 on v4

--- a/solution.py
+++ b/solution.py
@@ -104,28 +104,6 @@
 
     cin[...] = jnp.zeros(cin.shape, BF16)
 
-    @pl.when(px == 0)
-    def _():
-        src0[0] = jnp.zeros(src0.shape[1:], BF16)
-        src1[0] = jnp.zeros(src1.shape[1:], BF16)
-
-    @pl.when(px == n_gx - 1)
-    def _():
-        src0[3] = jnp.zeros(src0.shape[1:], BF16)
-        src1[2] = jnp.zeros(src1.shape[1:], BF16)
-
-    @pl.when(py == 0)
-    def _():
-        src0[:, 0] = jnp.zeros((4, 64, 256), BF16)
-        src1[:, 0] = jnp.zeros((3, 32, 256), BF16)
-        cin[0] = jnp.zeros(cin.shape[1:], BF16)
-
-    @pl.when(py == n_gy - 1)
-    def _():
-        src0[:, 5] = jnp.zeros((4, 64, 256), BF16)
-        src1[:, 3] = jnp.zeros((3, 32, 256), BF16)
-        cin[2] = jnp.zeros(cin.shape[1:], BF16)
-
     barrier = pltpu.get_barrier_semaphore()
     greeted = 0
     coarse_moves = [(far_dx, 0), (2, 0), (-2, 0), (1, 0), (-1, 0)]
@@ -135,6 +113,26 @@
         @pl.when(exists(dx, dy))
         def _():
             pl.semaphore_signal(barrier, inc=1, device_id=device(dx, dy), device_id_type=MESH)
+
+    @pl.when(px == 0)
+    def _():
+        src0[0] = jnp.zeros(src0.shape[1:], BF16)
+        src1[0] = jnp.zeros(src1.shape[1:], BF16)
+
+    @pl.when(px == n_gx - 1)
+    def _():
+        src0[3] = jnp.zeros(src0.shape[1:], BF16)
+        src1[2] = jnp.zeros(src1.shape[1:], BF16)
+
+    @pl.when(py == 0)
+    def _():
+        src0[:, 0] = jnp.zeros((4, 64, 256), BF16)
+        src1[:, 0] = jnp.zeros((3, 32, 256), BF16)
+
+    @pl.when(py == n_gy - 1)
+    def _():
+        src0[:, 5] = jnp.zeros((4, 64, 256), BF16)
+        src1[:, 3] = jnp.zeros((3, 32, 256), BF16)
 
     used = []
     waits = []
@@ -176,29 +174,27 @@
         row1, halo1 = (2, 0) if dy == 1 else (1, 3)
         leaf_y[dy] = message(src0.at[pl.ds(1, 2), row], src0.at[pl.ds(1, 2), halo], 0, dy)
         mid_y[dy] = message(src1.at[1, row1], src1.at[1, halo1], 0, dy)
-        coarse_y[dy] = message(cin.at[1], cin.at[1 - dy], 0, dy)
+        coarse_y[dy] = message(cin.at[2 + parity, 1], cin.at[2 + parity, 1 - dy], 0, dy)
         for dx in SIDES:
             column = 0 if dx == 1 else 3
             leaf_xy[dx, dy] = message(src0.at[column, row], src0.at[column, halo], 0, dy, -dx)
             mid_xy[dx, dy] = message(src1.at[1 - dx, row1], src1.at[1 - dx, halo1], 0, dy, -dx)
     coarse_x = []
-    own = cin.at[1, 2 + parity]
     for dx, dy in coarse_moves:
         slot = (2 - dx) + lax.rem(px + (dx + n_gx), 2)
-        target = cin.at[1 - dy, slot]
-        coarse_x.append(message(own, target, dx, dy, came_sem=coarse_came.at[1 - dy, slot]))
+        coarse_x.append(message(cin.at[2 + parity], cin.at[slot], dx, 0, came_sem=coarse_came.at[slot]))
     coarse_arrivals = []
     for dx, dy in coarse_moves:
         slot = dx + 2 + parity
         copy = pltpu.make_async_remote_copy(
-            src_ref=own,
-            dst_ref=cin.at[1 + dy, slot],
+            src_ref=cin.at[2 + parity],
+            dst_ref=cin.at[slot],
             send_sem=sent.at[0],
-            recv_sem=coarse_came.at[1 + dy, slot],
-            device_id=device(dx, dy),
+            recv_sem=coarse_came.at[slot],
+            device_id=device(dx, 0),
             device_id_type=MESH,
         )
-        coarse_arrivals.append((copy, None, exists(dx, dy)))
+        coarse_arrivals.append((copy, None, exists(dx, 0)))
 
     for copy in weight_copies:
         copy.wait()
@@ -265,18 +261,18 @@
         src1[1, 1:3, :, sz * 128 : (sz + 1) * 128] = made[:, :128].astype(BF16).reshape(2, 32, 128)
         total = made[:, 128:] if sz == 0 else total + made[:, 128:]
     level2 = total.reshape(2, 2, 16, 64)
+    pl.semaphore_wait(barrier, greeted)
+    for dx in SIDES:
+        start(mid_x[dx])
+    for dy in SIDES:
+        start(mid_y[dy])
     pieces = []
     for sz in range(2):
         high, low = split(jnp.concatenate([level2[0, sz], level2[1, sz]], axis=1))
         pieces.append(dot3(high, low, wup_ref[0, 0, 0:64, 0:128], wup_ref[0, 1, 0:64, 0:128]))
-    cin[1, 2 + parity] = jnp.concatenate(pieces, axis=1).astype(BF16)
-    pl.semaphore_wait(barrier, greeted)
-    for item in coarse_x:
-        start(item)
-    for dx in SIDES:
-        start(mid_x[dx])
-    for dy in SIDES:
-        start(mid_y[dy])
+    cin[2 + parity, 1] = jnp.concatenate(pieces, axis=1).astype(BF16)
+    for dy in SIDES:
+        start(coarse_y[dy])
     for first in (4, 1, 2):
         for dx in SIDES:
             start(leaf_x[dx, first])
@@ -339,6 +335,14 @@
         )
 
     for dy in SIDES:
+        arrive(coarse_y[dy])
+    for item in coarse_x:
+        start(item)
+    for dx in SIDES:
+        arrive(mid_x[dx])
+        for dy in SIDES:
+            start(mid_xy[dx, dy])
+    for dy in SIDES:
         arrive(leaf_y[dy])
         arrive(mid_y[dy])
     for mz in range(3):
@@ -356,14 +360,6 @@
         acc_ref[mz] = acc
         acc1_ref[mz] = acc1
 
-    for item in coarse_arrivals:
-        arrive(item)
-    for dy in SIDES:
-        start(coarse_y[dy])
-    for dx in SIDES:
-        arrive(mid_x[dx])
-        for dy in SIDES:
-            start(mid_xy[dx, dy])
     for first in (4, 1):
         for dx in SIDES:
             arrive(leaf_x[dx, first])
@@ -403,15 +399,16 @@
     twice_high = jnp.concatenate([wd_high[k * 64 : k * 64 + 64] for k in (0, 0, 1, 1, 2, 2, 3, 3)], axis=0)
     twice_low = jnp.concatenate([wd_low[k * 64 : k * 64 + 64] for k in (0, 0, 1, 1, 2, 2, 3, 3)], axis=0)
 
-    for dy in SIDES:
-        arrive(coarse_y[dy])
+    for item in coarse_arrivals:
+        arrive(item)
+    for dy in SIDES:
         for dx in SIDES:
             arrive(mid_xy[dx, dy])
     own_side = pl.ds(pl.multiple_of(parity * 64, 64), 64)
     acc = None
     for mx in range(3):
         for my in range(3):
-            one, two = cin[my, 2 * mx], cin[my, 2 * mx + 1]
+            one, two = cin[2 * mx, my], cin[2 * mx + 1, my]
             coarse = jnp.concatenate([one[:, :64], two[:, :64], one[:, 64:], two[:, 64:]], axis=1)
             wanted = jnp.concatenate(
                 [
@@ -503,7 +500,7 @@
             pltpu.VMEM((2, 512, 256), BF16),
             pltpu.VMEM((4, 6, 64, 256), BF16),
             pltpu.VMEM((3, 4, 32, 256), BF16),
-            pltpu.VMEM((3, 6, 16, 128), BF16),
+            pltpu.VMEM((6, 3, 16, 128), BF16),
             pltpu.VMEM((3, 3, 7, 128, 128), BF16),
             pltpu.VMEM((2, 2, 192, 256), BF16),
             pltpu.VMEM((2, 256, 256), BF16),
@@ -515,7 +512,7 @@
             pltpu.SemaphoreType.DMA((3,)),
             pltpu.SemaphoreType.DMA((MESSAGES,)),
             pltpu.SemaphoreType.DMA((MESSAGES,)),
-            pltpu.SemaphoreType.DMA((3, 6)),
+            pltpu.SemaphoreType.DMA((6,)),
         ],
         compiler_params=pltpu.CompilerParams(
             collective_id=0, has_side_effects=True, vmem_limit_bytes=48 * 1024 * 1024

time: 18.4 us -> 18.3 us (level)
  the two profiles are of different devices: /device:TPU:111 before, /device:TPU:152 now
where the time goes in v5:
time: 18.3 us; the launch traced here: 18.2 us
  Pallas kernels  17.2 us (94%)
  local copies, waits for them, and re-layouts  0.97 us (5%)
    pallas_call x1, Pallas kernels, per_device(): made(*(pltpu.with_memory_space_constraint(operand, pltpu.HBM) for operand...  17.2 us
    unnamed x1, local copies, waits for them, and re-layouts  0.97 us

profile of v5, /device:TPU:152, one launch (start us, length us, event | category | flops | bytes accessed | tf_op | source)
XLA Modules:
  0.0 18.2 jit_solution(15812390214959987053)
XLA Ops:
  0.0 17.2 %far_field.1 = f32[2048,128]{1,0:T(8,128)S(1)} custom-call(f32[64,32,128]{2,1,0:T(8,128)} %bitcast.5, bf16[32,32,316]{2,1,0:T(8,128)(2,1)} %bitcast.6, f32[32,64]{1,0:T(8,128)} %pin_hbm.1, f32[32,64]{1,0:T(8,128)} %bitcast.7, f32[8,64,64]{2,1,0:T(8,128)} %m2m_hbm.1), custom_call_target="tpu_custom_call" | custom-call | tf_op jit(solution)/shard_map/far_field/pallas_call | solution.py:523
  17.2 1.0 %copy.7 = f32[64,4,8,128]{3,2,1,0:T(8,128)} copy(f32[64,4,8,128]{3,2,1,0:T(8,128)S(1)} %bitcast.4) | data formatting | bytes 2097152

commit v6 on v5

--- a/solution.py
+++ b/solution.py
@@ -209,7 +209,7 @@
         wup_ref[sz, 0] = high
         wup_ref[sz, 1] = low
 
-    flat_ref = x_ref.reshape(3072, 128)
+    flat_ref = x_ref.reshape(4608, 128)
     for X in range(2):
         x_copies[X].wait()
         for Y in range(4):
@@ -223,8 +223,8 @@
                 axis=0,
             )
             turned = block.T
-            turn_ref[parent, 0] = turned[:, :128]
-            turn_ref[parent, 1] = turned[:, 128:]
+            turn_ref[parent, 0, 0:128] = turned[:, :128]
+            turn_ref[parent, 1, 0:128] = turned[:, 128:]
             for sz in range(2):
                 high, low = split(
                     jnp.concatenate(
@@ -492,10 +492,10 @@
             pltpu.VMEM((32, 64), F32),
             pltpu.VMEM((32, 64), F32),
             pltpu.VMEM((8, 64, 64), F32),
-            pltpu.VMEM((2, 64, 24, 128), F32),
+            pltpu.VMEM((3, 64, 24, 128), F32),
             pltpu.VMEM((32, 32, 316), BF16),
-            pltpu.VMEM((344 * 8, 128), F32),
-            pltpu.VMEM((8, 2, 128, 128), F32),
+            pltpu.VMEM((344 * 9, 128), F32),
+            pltpu.VMEM((8, 2, 136, 128), F32),
             pltpu.VMEM((2, 512, 256), BF16),
             pltpu.VMEM((2, 512, 256), BF16),
             pltpu.VMEM((4, 6, 64, 256), BF16),
@@ -506,7 +506,7 @@
             pltpu.VMEM((2, 256, 256), BF16),
             pltpu.VMEM((3, 512, 256), F32),
             pltpu.VMEM((3, 64, 256), F32),
-            pltpu.VMEM((32 * 72, 128), F32),
+            pltpu.VMEM((33 * 72, 128), F32),
             pltpu.SemaphoreType.DMA((2,)),
             pltpu.SemaphoreType.DMA,
             pltpu.SemaphoreType.DMA((3,)),

time: 18.3 us -> 18.3 us (level)
  no operation moved by 1% of the time
where the time goes in v6:
time: 18.3 us; the launch traced here: 18.2 us
  Pallas kernels  17.2 us (94%)
  local copies, waits for them, and re-layouts  0.97 us (5%)
    pallas_call x1, Pallas kernels, per_device(): made(*(pltpu.with_memory_space_constraint(operand, pltpu.HBM) for operand...  17.2 us
    unnamed x1, local copies, waits for them, and re-layouts  0.97 us

profile of v6, /device:TPU:152, one launch (start us, length us, event | category | flops | bytes accessed | tf_op | source)
XLA Modules:
  0.0 18.2 jit_solution(2323260100405833605)
XLA Ops:
  0.0 17.2 %far_field.1 = f32[2048,128]{1,0:T(8,128)S(1)} custom-call(f32[64,32,128]{2,1,0:T(8,128)} %bitcast.5, bf16[32,32,316]{2,1,0:T(8,128)(2,1)} %bitcast.6, f32[32,64]{1,0:T(8,128)} %pin_hbm.1, f32[32,64]{1,0:T(8,128)} %bitcast.7, f32[8,64,64]{2,1,0:T(8,128)} %m2m_hbm.1), custom_call_target="tpu_custom_call" | custom-call | tf_op jit(solution)/shard_map/far_field/pallas_call | solution.py:523
  17.2 1.0 %copy.7 = f32[64,4,8,128]{3,2,1,0:T(8,128)} copy(f32[64,4,8,128]{3,2,1,0:T(8,128)S(1)} %bitcast.4) | data formatting | bytes 2097152

commit v7 on v6

--- a/solution.py
+++ b/solution.py
@@ -100,7 +100,6 @@
     for copy in x_copies:
         copy.start()
     ops_copy = pltpu.make_async_copy(ops_hbm, ops_ref, ops_sem)
-    ops_copy.start()
 
     cin[...] = jnp.zeros(cin.shape, BF16)
 
@@ -212,6 +211,8 @@
     flat_ref = x_ref.reshape(4608, 128)
     for X in range(2):
         x_copies[X].wait()
+        if X == 1:
+            ops_copy.start()
         for Y in range(4):
             parent = X * 4 + Y
             block = jnp.concatenate(

time: 18.3 us -> 18.3 us (level)
  no operation moved by 1% of the time
where the time goes in v7:
time: 18.3 us; the launch traced here: 18.2 us
  Pallas kernels  17.2 us (94%)
  local copies, waits for them, and re-layouts  0.97 us (5%)
    pallas_call x1, Pallas kernels, per_device(): made(*(pltpu.with_memory_space_constraint(operand, pltpu.HBM) for operand...  17.2 us
    unnamed x1, local copies, waits for them, and re-layouts  0.97 us

profile of v7, /device:TPU:152, one launch (start us, length us, event | category | flops | bytes accessed | tf_op | source)
XLA Modules:
  0.0 18.2 jit_solution(7940848596676144382)
XLA Ops:
  0.0 17.2 %far_field.1 = f32[2048,128]{1,0:T(8,128)S(1)} custom-call(f32[64,32,128]{2,1,0:T(8,128)} %bitcast.5, bf16[32,32,316]{2,1,0:T(8,128)(2,1)} %bitcast.6, f32[32,64]{1,0:T(8,128)} %pin_hbm.1, f32[32,64]{1,0:T(8,128)} %bitcast.7, f32[8,64,64]{2,1,0:T(8,128)} %m2m_hbm.1), custom_call_target="tpu_custom_call" | custom-call | tf_op jit(solution)/shard_map/far_field/pallas_call | solution.py:524
  17.2 1.0 %copy.7 = f32[64,4,8,128]{3,2,1,0:T(8,128)} copy(f32[64,4,8,128]{3,2,1,0:T(8,128)S(1)} %bitcast.4) | data formatting | bytes 2097152
